TPU v7x, 32 devices: a whole 2x2x4 slice. The times are simulated.
32 devices in a mesh: cuts: 4 (over y, core), grid: 8 (over z, x).
Axes of the slice: x: 2, y: 2, z: 4, core: 2. Of those that a mesh axis runs over, the one named last changes fastest.
Arguments:
- orbitals: bfloat16 [32768, 1024], P('grid', 'cuts'), may hold values from -9 to 9, as said below
- potential: float32 [32768], P('grid'), may hold values from -1 to 1
- core_density: float32 [32768], P('grid'), may hold values from 0.05 to 0.5
- occupation: int32 [1024], P('cuts'), may hold values from 0 to 2
- slice_counts: int32 [4], P('cuts'), may hold values from 128 to 256
Outputs:
- orbitals_out: bfloat16 [32768, 1024], P('grid', 'cuts')
- potential_out: float32 [32768], P('grid')
Inputs may be any that keep to these rules, and one draw needn't show every extreme that they name: `orbitals`: every entry has magnitude at most 9.
All inputs are finite; a program needn't handle non-finite values.
Results may differ from a plain program's by a relative error of at most 0.0015.
The roundings to bfloat16 on the way count: a program that leaves them out, or rounds other values in their place, can miss the bound.
Values may be sent and summed in bfloat16 or wider, within the bound.
A program may use at most 64 MiB of HBM per device.

v0:
```python
import jax
import jax.numpy as jnp
from jax import lax
from jax.sharding import PartitionSpec as P

mixing = 0.3
step_size = 0.5


def with_halo(x, sides, width):
    for axis, dim in sides:
        peers, length = (lax.axis_size(axis), x.shape[dim])
        up = [(i, (i + 1) % peers) for i in range(peers)]
        down = [(j, i) for i, j in up]
        last = lax.slice_in_dim(x, length - width, length, axis=dim)
        leading = lax.slice_in_dim(x, 0, width, axis=dim)
        before = lax.ppermute(last, axis, up)
        after = lax.ppermute(leading, axis, down)
        x = jnp.concatenate([before, x, after], axis=dim)
    return x


def per_device(orbitals, potential, core_density, occupation, slice_counts):
    highest = lax.Precision.HIGHEST
    coefficient = (3.0 / jnp.pi) ** (1.0 / 3.0)
    rows = orbitals.shape[0]
    width = orbitals.shape[1]
    total_points = rows * lax.axis_size("grid")
    total_states = width * lax.axis_size("cuts")
    padded = with_halo(orbitals, (("grid", 0),), 1).astype(jnp.float32)
    middle = padded[1:-1]
    kinetic = -0.5 * (padded[2:] + padded[:-2] - 2.0 * middle)
    applied = (kinetic + potential[:, None] * middle).astype(jnp.bfloat16)
    stacked = jnp.concatenate([orbitals, applied], axis=1)
    contract = (((0,), (0,)), ((), ()))
    partial_sums = lax.dot_general(orbitals, stacked, contract, preferred_element_type=jnp.float32)
    summed = lax.psum(partial_sums, "grid")
    intersection = summed[:, :width] / total_points
    ritz = summed[:, width:] / total_points
    factor = jnp.linalg.cholesky(intersection)
    identity = jnp.eye(width, dtype=jnp.float32)
    inverse = lax.linalg.triangular_solve(factor, identity, left_side=True, lower=True)
    projected = jnp.dot(jnp.dot(inverse, ritz, precision=highest), inverse.T, precision=highest)
    rotation = jnp.dot(inverse.T, identity - step_size * projected, precision=highest).astype(
        jnp.bfloat16
    )
    rotated = jnp.dot(orbitals, rotation, preferred_element_type=jnp.float32)
    orbitals_out = rotated.astype(jnp.bfloat16)
    live = (jnp.arange(width) < slice_counts[0]).astype(jnp.float32)
    weights = occupation.astype(jnp.float32) * live / (2.0 * total_states)
    contribution = jnp.sum(rotated * rotated * weights[None, :], axis=1)
    density = core_density + lax.psum(contribution, "cuts")
    potential_out = (1.0 - mixing) * potential + mixing * (-coefficient * jnp.cbrt(density))
    return (orbitals_out, potential_out)


def solution(mesh):
    placed = (P("grid", "cuts"), P("grid"), P("grid"), P("cuts"), P("cuts"))
    return jax.shard_map(
        per_device,
        mesh=mesh,
        in_specs=placed,
        out_specs=(P("grid", "cuts"), P("grid")),
        check_vma=False,
    )
```

profile of v0, /device:TPU:0, one launch (start us, length us, event | category | flops | bytes accessed | tf_op | source)
XLA Modules:
  0.0 198.1 jit_solution(1708575823228396398)
XLA Ops:
  7.2 0.0 all-reduce.3.cloned.1.call-start
  7.2 0.7 fusion.30
  7.9 2.9 %collective-permute-start = (bf16[1,256]{1,0:T(2,128)(2,1)S(1)}, bf16[1,256]{1,0:T(2,128)(2,1)S(1)}, u32[]{:S(2)}, u32[]{:S(2)}) collective-permute-start(bf16[1,256]{1,0:T(2,128)(2,1)S(1)} %get-tuple-element.25), channel_id=1, source_target_pairs={{0,1},{1,2},{2,3},{3,4},{4,5},{5,6},{6,7},{7,0},{8,9},{9,10},{10,1... | collective-permute-start | bytes 1544 | tf_op jit(solution)/shard_map/ppermute | solution.py:17
  10.9 3.1 %collective-permute-start.1 = (bf16[1,256]{1,0:T(2,128)(2,1)S(1)}, bf16[1,256]{1,0:T(2,128)(2,1)S(1)}, u32[]{:S(2)}, u32[]{:S(2)}) collective-permute-start(bf16[1,256]{1,0:T(2,128)(2,1)S(1)} %get-tuple-element.24), channel_id=1, source_target_pairs={{1,0},{2,1},{3,2},{4,3},{5,4},{6,5},{7,6},{0,7},{9,8},{10,9},{11,1... | collective-permute-start | bytes 1544 | tf_op jit(solution)/shard_map/ppermute | solution.py:18
  14.6 0.9 collective-permute-done
  15.4 0.0 collective-permute-done.1
  15.4 9.2 %concatenate.8 = bf16[4098,256]{1,0:T(8,128)(2,1)S(1)} concatenate(bf16[1,256]{1,0:T(2,128)(2,1)S(1)} %collective-permute-done, bf16[4096,256]{1,0:T(8,128)(2,1)} %param.5, bf16[1,256]{1,0:T(2,128)(2,1)S(1)} %collective-permute-done.1), dimensions={0} | concatenate | bytes 4196352 | tf_op jit(solution)/shard_map/concatenate | solution.py:19
  24.7 0.3 convert_element_type.24
  25.0 0.4 copy-done.2
  25.4 1.5 fusion.3
  26.9 0.0 copy-done
  27.0 2.1 %fusion.8 = f32[256,512]{0,1:T(8,128)} fusion(bf16[4096,256]{1,0:T(8,128)(2,1)S(1)} %copy-done, bf16[4096,256]{1,0:T(8,128)(2,1)S(1)} %fusion.3), kind=kOutput, calls=%fused_computation.13 | convolution fusion | flops 1082130432 | bytes 4718592 | tf_op jit(solution)/shard_map/dot_general | solution.py:36
  29.1 0.0 all-reduce.3.cloned.1.call-update
  29.1 0.6 iota_multiply_fusion
  29.7 0.0 copy-done.4
  29.7 0.6 fusion.23
  30.3 72.9 %all-reduce.3.cloned.1.call-done = f32[256,512]{0,1:T(8,128)} async-done(((f32[256,512]{0,1:T(8,128)}), f32[256,512]{0,1:T(8,128)}) %all-reduce.3.cloned.1.call-update) | async-done | bytes 524304 | tf_op jit(solution)/shard_map/psum | solution.py:37
  103.2 1.0 slice_multiply_fusion.2
  104.2 0.1 copy.7
  104.4 1.0 fusion.13
  105.4 11.7 %cholesky.50 = f32[128,128]{1,0:T(8,128)S(1)} custom-call(f32[128,128]{1,0:T(8,128)S(1)} %cholesky.118), custom_call_target="Cholesky" | custom-call | tf_op jit(solution)/shard_map/jit(cholesky)/cholesky | solution.py:40
  117.1 0.6 select_reduce_fusion.1
  117.7 10.4 %custom-call.14 = f32[1,128,128]{1,2,0:T(8,128)} custom-call(f32[1,128,128]{2,1,0:T(8,128)S(1)} %get-tuple-element.29), custom_call_target="InvertDiagBlocksLowerTriangular" | custom-call | tf_op jit(solution)/shard_map/jit(cholesky)/cholesky | solution.py:40
  128.1 1.0 constant_dynamic-update-slice_fusion.1
  129.2 0.9 convolution_subtract_fusion.1
  130.1 12.5 %cholesky.105 = f32[128,128]{1,0:T(8,128)S(1)} custom-call(f32[128,128]{1,0:T(8,128)} %convolution_subtract_fusion.1), custom_call_target="Cholesky" | custom-call | tf_op jit(solution)/shard_map/jit(cholesky)/cholesky | solution.py:40
  142.7 1.3 compare_reduce_fusion
  145.2 0.7 triangular_solve.63
  146.0 5.1 %while.1 = (s32[]{:T(128)}, f32[256,256]{1,0:T(8,128)S(1)}, s32[2,2]{1,0:T(2,128)S(1)}, f32[2,128,128]{2,1,0:T(8,128)}, s32[]{:T(128)}) while((s32[]{:T(128)}, f32[256,256]{1,0:T(8,128)S(1)}, s32[2,2]{1,0:T(2,128)S(1)}, f32[2,128,128]{2,1,0:T(8,128)}, s32[]{:T(128)}) %tuple.30), condition=%wide.while_cond, body=%wide.while_body.sunk | while | flops 2 | bytes 132705 | solution.py:42
  146.0 0.6 fusion.41
  146.6 2.0 %bitcast_dynamic-update-slice_fusion.2 = f32[2,128,128]{2,1,0:T(8,128)} fusion(f32[2,128,128]{2,1,0:T(8,128)} %get-tuple-element.71, s32[]{:T(128)} %get-tuple-element.68, f32[256,256]{1,0:T(8,128)S(1)} %get-tuple-element.74, s32[]{:T(128)} %bitcast.39, s32[]{:T(128)} %bitcast.40), kind=kLoop, calls=%fused_computation.clone.1 | loop fusion | bytes 132608 | tf_op jit(solution)/shard_map/triangular_solve
  148.5 0.6 fusion.41
  149.1 2.0 bitcast_dynamic-update-slice_fusion.2
  151.1 20.5 %custom-call.15 = f32[2,128,128]{1,2,0:T(8,128)S(1)} custom-call(f32[2,128,128]{2,1,0:T(8,128)} %get-tuple-element.9), custom_call_target="InvertDiagBlocksLowerTriangular" | custom-call | tf_op jit(solution)/shard_map/triangular_solve | solution.py:42
  171.6 0.3 fusion.15
  171.9 0.3 convolution_subtract_fusion
  172.1 0.3 fusion.19
  172.5 0.0 copy-done.1
  172.5 0.4 fusion.12
  172.9 0.4 fusion.11
  173.3 0.6 convolution_convert_fusion
  173.9 0.0 copy-done.5
  173.9 0.0 copy-start.3
  173.9 2.6 %multiply_reduce_fusion = (f32[4096]{0:T(1024)S(1)}, bf16[4096,256]{0,1:T(8,128)(2,1)}) fusion(f32[256]{0:T(256)S(1)} %copy-done.5, bf16[256,256]{1,0:T(8,128)(2,1)S(1)} %convolution_convert_fusion, bf16[4096,256]{1,0:T(8,128)(2,1)S(1)} %copy-done), kind=kOutput, calls=%fused_computation.11 | convolution fusion | flops 541061120 | bytes 4342784 | tf_op jit(solution)/shard_map/dot_general | solution.py:47
  176.5 4.1 %copy.8 = bf16[4096,256]{1,0:T(8,128)(2,1)} copy(bf16[4096,256]{0,1:T(8,128)(2,1)} %get-tuple-element.23) | data formatting | bytes 4194304
  180.6 10.1 %psum.15 = f32[4096]{0:T(1024)S(1)} all-reduce(f32[4096]{0:T(1024)S(1)} %get-tuple-element.22), channel_id=1, replica_groups=mesh['cuts'=4,'grid'=8] {'cuts'}, use_global_device_ids=true, to_apply=%region_6.7 | all-reduce | flops 4096 | bytes 32768 | tf_op jit(solution)/shard_map/psum | solution.py:52
  190.7 0.0 copy-done.3
  190.7 0.6 multiply_add_fusion
  (14 shorter events, 0.2 us)
Async XLA Ops:
  7.2 96.0 %all-reduce.3.cloned.1.call-start = ((), (), s32[]{:S(2)}) async-start(), calls=%async_computation | async-start | bytes 1048576 | tf_op jit(solution)/shard_map/psum | solution.py:37
  7.9 7.5 %collective-permute-start = (bf16[1,256]{1,0:T(2,128)(2,1)S(1)}, bf16[1,256]{1,0:T(2,128)(2,1)S(1)}, u32[]{:S(2)}, u32[]{:S(2)}) collective-permute-start(bf16[1,256]{1,0:T(2,128)(2,1)S(1)} %get-tuple-element.25), channel_id=1, source_target_pairs={{0,1},{1,2},{2,3},{3,4},{4,5},{5,6},{6,7},{7,0},{8,9},{9,10},{10,1... | collective-permute-start | bytes 1544 | tf_op jit(solution)/shard_map/ppermute | solution.py:17
  10.9 4.6 %collective-permute-start.1 = (bf16[1,256]{1,0:T(2,128)(2,1)S(1)}, bf16[1,256]{1,0:T(2,128)(2,1)S(1)}, u32[]{:S(2)}, u32[]{:S(2)}) collective-permute-start(bf16[1,256]{1,0:T(2,128)(2,1)S(1)} %get-tuple-element.24), channel_id=1, source_target_pairs={{1,0},{2,1},{3,2},{4,3},{5,4},{6,5},{7,6},{0,7},{9,8},{10,9},{11,1... | collective-permute-start | bytes 1544 | tf_op jit(solution)/shard_map/ppermute | solution.py:18
  24.7 0.7 copy-start.2
  25.4 1.6 copy-start
  27.0 2.7 %copy-start.4 = (s32[256]{0:T(256)S(1)}, s32[256]{0:T(256)}, u32[]{:S(2)}) copy-start(s32[256]{0:T(256)} %param.8) | copy-start | bytes 3076
  103.2 69.3 %copy-start.1 = (f32[256,512]{0,1:T(8,128)S(1)}, f32[256,512]{0,1:T(8,128)}, u32[]{:S(2)}) copy-start(f32[256,512]{0,1:T(8,128)} %all-reduce.3.cloned.1.call-done) | copy-start | bytes 1572868
  142.7 31.2 %copy-start.5 = (f32[256]{0:T(256)S(1)}, f32[256]{0:T(256)}, u32[]{:S(2)}) copy-start(f32[256]{0:T(256)} %fusion.23) | copy-start | bytes 3076
  173.9 16.7 %copy-start.3 = (f32[4096]{0:T(1024)S(1)}, f32[4096]{0:T(1024)}, u32[]{:S(2)}) copy-start(f32[4096]{0:T(1024)} %param.7) | copy-start | bytes 49156
Sparse Core Ops, SparseCore 0:
  29.2 73.9 all-reduce.2
where the time goes:
time: 199 us; the launch traced here: 198 us
  waiting for transfers between devices  73.8 us (37%)
  other arithmetic  62.8 us (32%)
  local copies, waits for them, and re-layouts  20.5 us (10%)
  between operations  16.1 us (8%)
  blocking collectives  10.1 us (5%)
  matrix products  8.85 us (4%)
  starting transfers between devices  6.05 us (3%)
    psum x1, waiting for transfers between devices, per_device(): summed = lax.psum(partial_sums, 'grid')  72.9 us
    another operation x6, other arithmetic, per_device(): factor = jnp.linalg.cholesky(intersection)  36.6 us
    another operation x3, other arithmetic, per_device(): lax.linalg.triangular_solve(factor, identity, left_side=True, lower=True)  21.1 us
    psum x1, blocking collectives, per_device(): density = core_density + lax.psum(contribution, 'cuts')  10.1 us
    concatenate x1, local copies, waits for them, and re-layouts, with_halo(): x = jnp.concatenate([before, x, after], axis=dim)  9.22 us
    another operation x6, local copies, waits for them, and re-layouts  5.15 us
    unnamed x13, local copies, waits for them, and re-layouts  4.51 us
  transfers between devices with their start and end apart: 3, of which 2 were waited for; matrix products, arithmetic and copies ran while one was open for 1% of the time, Pallas kernels for 0%

commit v1 on v0

v1 whole, which is shorter than its diff:
```python
import functools

import jax
import jax.numpy as jnp
from jax import lax
from jax.experimental import pallas as pl
from jax.experimental.pallas import tpu as pltpu
from jax.sharding import PartitionSpec as P

mixing = 0.3
step_size = 0.5
lanes = 128
halo = 16
block = 32
panel = 8
columns = (((0,), (0,)), ((), ()))
across = (((1,), (1,)), ((), ()))
highest = lax.Precision.HIGHEST


def three_parts(x):
    high = x.astype(jnp.bfloat16)
    rest = x - high.astype(jnp.float32)
    middle = rest.astype(jnp.bfloat16)
    low = (rest - middle.astype(jnp.float32)).astype(jnp.bfloat16)
    return high, middle, low


def eliminate(left, right):
    size = left.shape[0]
    rows = lax.broadcasted_iota(jnp.int32, (size, lanes), 0)
    tiles = [left[:, i : i + lanes] for i in range(0, left.shape[1], lanes)]
    tiles += [right[:, i : i + lanes] for i in range(0, right.shape[1], lanes)]
    for first in range(0, size, panel):
        spread = [
            jnp.broadcast_to(tiles[0][:, c : c + 1], (size, lanes))
            for c in range(first, first + panel)
        ]
        for step in range(panel):
            j = first + step
            column = spread[step]
            factor = column * (1.0 / column[j : j + 1, :])
            factor = jnp.where(rows > j, factor, 0.0)
            for c in range(step + 1, panel):
                spread[c] = spread[c] - factor * spread[c][j : j + 1, :]
            tiles = [t - factor * t[j : j + 1, :] for t in tiles]
    at = lax.broadcasted_iota(jnp.int32, (size, lanes), 1)
    pivots = jnp.sum(jnp.where(rows == at, tiles[0], 0.0), axis=1, keepdims=True)
    scale = lax.rsqrt(pivots)
    scale = scale * (1.5 - 0.5 * pivots * scale * scale)
    tiles = [t * scale for t in tiles]
    half = left.shape[1] // lanes
    return jnp.concatenate(tiles[:half], axis=1), jnp.concatenate(tiles[half:], axis=1)


def kernel(
    groups,
    slices,
    psi_hbm,
    potential_ref,
    occupation_ref,
    count_ref,
    rotation_ref,
    density_ref,
    psi,
    applied,
    gram,
    landed,
    summed,
    work,
    inverse_ref,
    mine,
    shares,
    load_sem,
    halo_send,
    halo_recv,
    scatter_send,
    scatter_recv,
    gather_send,
    gather_recv,
    share_send,
    share_recv,
):
    points, width = psi_hbm.shape
    me = lax.axis_index("grid")
    cut = lax.axis_index("cuts")
    part = width // groups
    chunk = lanes * 8
    total_points = points * groups

    load = pltpu.make_async_copy(psi_hbm, psi.at[pl.ds(halo, points)], load_sem)
    load.start()
    barrier = pltpu.get_barrier_semaphore()
    for d in range(1, groups):
        pl.semaphore_signal(
            barrier, inc=1, device_id={"grid": lax.rem(me + d, groups)}, device_id_type=pl.DeviceIdType.MESH
        )
    for d in range(1, slices):
        pl.semaphore_signal(
            barrier, inc=1, device_id={"cuts": lax.rem(cut + d, slices)}, device_id_type=pl.DeviceIdType.MESH
        )
    load.wait()

    gram[0] = jnp.zeros((width, width), jnp.float32)
    gram[1] = jnp.zeros((width, width), jnp.float32)

    def overlap(i, carry):
        x = psi[pl.ds(pl.multiple_of(i * chunk, chunk) + halo, chunk), :]
        gram[0] += lax.dot_general(x, x, columns, preferred_element_type=jnp.float32)
        return carry

    lax.fori_loop(0, points // chunk, overlap, 0)
    pl.semaphore_wait(barrier, groups + slices - 2)

    up = pltpu.make_async_remote_copy(
        src_ref=psi_hbm.at[pl.ds(points - halo, halo)],
        dst_ref=psi.at[pl.ds(0, halo)],
        send_sem=halo_send.at[0],
        recv_sem=halo_recv.at[0],
        device_id={"grid": lax.rem(me + 1, groups)},
        device_id_type=pl.DeviceIdType.MESH,
    )
    down = pltpu.make_async_remote_copy(
        src_ref=psi_hbm.at[pl.ds(0, halo)],
        dst_ref=psi.at[pl.ds(points + halo, halo)],
        send_sem=halo_send.at[1],
        recv_sem=halo_recv.at[1],
        device_id={"grid": lax.rem(me + groups - 1, groups)},
        device_id_type=pl.DeviceIdType.MESH,
    )
    up.start()
    down.start()

    own = pl.ds(pl.multiple_of(me * part, part), part)

    def scatter(which):
        copies = []
        for d in range(1, groups):
            to = lax.rem(me + d, groups)
            copies.append(
                pltpu.make_async_remote_copy(
                    src_ref=gram.at[which, pl.ds(pl.multiple_of(to * part, part), part)],
                    dst_ref=landed.at[which, d - 1],
                    send_sem=scatter_send.at[which, d - 1],
                    recv_sem=scatter_recv.at[which, d - 1],
                    device_id={"grid": to},
                    device_id_type=pl.DeviceIdType.MESH,
                )
            )
        for copy in copies:
            copy.start()
        return copies

    def gather(which, copies):
        for copy in copies:
            copy.wait()
        total = gram[which, own, :]
        for d in range(groups - 1):
            total = total + landed[which, d]
        summed[which, own, :] = total * (1.0 / total_points)
        copies = []
        for d in range(1, groups):
            copies.append(
                pltpu.make_async_remote_copy(
                    src_ref=summed.at[which, own],
                    dst_ref=summed.at[which, own],
                    send_sem=gather_send.at[which, d - 1],
                    recv_sem=gather_recv.at[which, d - 1],
                    device_id={"grid": lax.rem(me + d, groups)},
                    device_id_type=pl.DeviceIdType.MESH,
                )
            )
        for copy in copies:
            copy.start()
        return copies

    first = scatter(0)
    up.wait()
    down.wait()

    def ritz(i, carry):
        base = pl.multiple_of(i * chunk, chunk)
        values = potential_ref[pl.ds(pl.multiple_of(i * 8, 8), 8), :]
        for s in range(8):
            x = psi[pl.ds(base + s * lanes, lanes + 2 * halo), :].astype(jnp.float32)
            middle = x[halo : halo + lanes]
            before = x[halo - 1 : halo + lanes - 1]
            after = x[halo + 1 : halo + lanes + 1]
            local = jnp.broadcast_to(values[s : s + 1, :], (lanes, lanes)).T
            local = jnp.concatenate([local] * (width // lanes), axis=1)
            kinetic = -0.5 * (after + before - 2.0 * middle)
            applied[s * lanes : (s + 1) * lanes, :] = (kinetic + local * middle).astype(jnp.bfloat16)
        x = psi[pl.ds(base + halo, chunk), :]
        gram[1] += lax.dot_general(x, applied[...], columns, preferred_element_type=jnp.float32)
        return carry

    lax.fori_loop(0, points // chunk, ritz, 0)
    first = gather(0, first)
    second = scatter(1)

    row = lax.broadcasted_iota(jnp.int32, (width, width), 0)
    column = lax.broadcasted_iota(jnp.int32, (width, width), 1)
    identity = (row == column).astype(jnp.float32)
    for copy in first:
        copy.wait()
    work[:, :width] = summed[0]
    work[:, width:] = identity

    def factor(k, carry):
        here = pl.ds(pl.multiple_of(k * block, block), block)
        back = lax.rem(width - k * block, width)
        left = pltpu.roll(work[here, :width], back, 1)
        left, right = eliminate(left, work[here, width:])
        inverse_ref[here, :] = right
        left = pltpu.roll(left, k * block, 1)
        at = lax.broadcasted_iota(jnp.int32, (block, width), 1)
        left = jnp.where(at >= (k + 1) * block, left, 0.0)
        lh, lm, ll = three_parts(left)
        rh, rm, rl = three_parts(right)
        lhs = jnp.concatenate([lh, lh, lm, lh, ll, lm], axis=0)
        a = jnp.concatenate([lh, lm, lh, ll, lh, lm], axis=0)
        b = jnp.concatenate([rh, rm, rh, rl, rh, rm], axis=0)
        rhs = jnp.concatenate([a, b], axis=1)
        work[...] -= lax.dot_general(lhs, rhs, columns, preferred_element_type=jnp.float32)
        return carry

    blocks = width // block
    lax.fori_loop(0, blocks // 2, factor, 0)
    second = gather(1, second)
    lax.fori_loop(blocks // 2, blocks, factor, 0)
    for copy in second:
        copy.wait()

    inverse = inverse_ref[...]
    projected = jnp.dot(inverse, summed[1], precision=highest, preferred_element_type=jnp.float32)
    projected = lax.dot_general(
        projected, inverse, across, precision=highest, preferred_element_type=jnp.float32
    )
    rotation = lax.dot_general(
        inverse,
        identity - step_size * projected,
        columns,
        precision=highest,
        preferred_element_type=jnp.float32,
    ).astype(jnp.bfloat16)
    rotation_ref[...] = rotation

    state = lax.broadcasted_iota(jnp.int32, (1, width), 1)
    live = (state < count_ref[0]).astype(jnp.float32)
    weights = occupation_ref[...].astype(jnp.float32) * live / (2.0 * width * slices)

    def contribute(i, carry):
        x = psi[pl.ds(pl.multiple_of(i * chunk, chunk) + halo, chunk), :]
        rotated = jnp.dot(x, rotation_ref[...], preferred_element_type=jnp.float32)
        square = rotated * rotated * weights
        narrow = square[:, :lanes]
        for c in range(lanes, width, lanes):
            narrow = narrow + square[:, c : c + lanes]
        sums = [
            jnp.sum(narrow[s * lanes : (s + 1) * lanes].T, axis=0, keepdims=True) for s in range(8)
        ]
        mine[pl.ds(pl.multiple_of(i * 8, 8), 8), :] = jnp.concatenate(sums, axis=0)
        return carry

    lax.fori_loop(0, points // chunk, contribute, 0)
    copies = []
    for d in range(1, slices):
        copies.append(
            pltpu.make_async_remote_copy(
                src_ref=mine,
                dst_ref=shares.at[cut],
                send_sem=share_send.at[d - 1],
                recv_sem=share_recv.at[d - 1],
                device_id={"cuts": lax.rem(cut + d, slices)},
                device_id_type=pl.DeviceIdType.MESH,
            )
        )
    for copy in copies:
        copy.start()
    shares[cut] = mine[...]
    for copy in copies:
        copy.wait()
    total = shares[0]
    for c in range(1, slices):
        total = total + shares[c]
    density_ref[...] = total


def per_device(orbitals, potential, core_density, occupation, slice_counts):
    coefficient = (3.0 / jnp.pi) ** (1.0 / 3.0)
    points, width = orbitals.shape
    groups, slices = (lax.axis_size("grid"), lax.axis_size("cuts"))
    folded = (points // lanes, lanes)
    part = width // groups
    vmem = pl.BlockSpec(memory_space=pltpu.VMEM)
    rotation, contribution = pl.pallas_call(
        functools.partial(kernel, groups, slices),
        out_shape=(
            jax.ShapeDtypeStruct((width, width), jnp.bfloat16),
            jax.ShapeDtypeStruct(folded, jnp.float32),
        ),
        in_specs=[
            pl.BlockSpec(memory_space=pl.ANY),
            vmem,
            vmem,
            pl.BlockSpec(memory_space=pltpu.SMEM),
        ],
        out_specs=(vmem, vmem),
        scratch_shapes=[
            pltpu.VMEM((points + 2 * halo, width), jnp.bfloat16),
            pltpu.VMEM((8 * lanes, width), jnp.bfloat16),
            pltpu.VMEM((2, width, width), jnp.float32),
            pltpu.VMEM((2, groups - 1, part, width), jnp.float32),
            pltpu.VMEM((2, width, width), jnp.float32),
            pltpu.VMEM((width, 2 * width), jnp.float32),
            pltpu.VMEM((width, width), jnp.float32),
            pltpu.VMEM(folded, jnp.float32),
            pltpu.VMEM((slices,) + folded, jnp.float32),
            pltpu.SemaphoreType.DMA,
            pltpu.SemaphoreType.DMA((2,)),
            pltpu.SemaphoreType.DMA((2,)),
            pltpu.SemaphoreType.DMA((2, groups - 1)),
            pltpu.SemaphoreType.DMA((2, groups - 1)),
            pltpu.SemaphoreType.DMA((2, groups - 1)),
            pltpu.SemaphoreType.DMA((2, groups - 1)),
            pltpu.SemaphoreType.DMA((slices - 1,)),
            pltpu.SemaphoreType.DMA((slices - 1,)),
        ],
        compiler_params=pltpu.CompilerParams(
            collective_id=0, has_side_effects=True, vmem_limit_bytes=40 * 1024 * 1024
        ),
        cost_estimate=pl.CostEstimate(
            flops=8 * points * width * width, bytes_accessed=2 * points * width, transcendentals=0
        ),
    )(orbitals, potential.reshape(folded), occupation.reshape(1, width), slice_counts)
    rotated = jnp.dot(orbitals, rotation, preferred_element_type=jnp.float32)
    orbitals_out = rotated.astype(jnp.bfloat16)
    density = core_density + contribution.reshape(points)
    potential_out = (1.0 - mixing) * potential + mixing * (-coefficient * jnp.cbrt(density))
    return (orbitals_out, potential_out)


def solution(mesh):
    placed = (P("grid", "cuts"), P("grid"), P("grid"), P("cuts"), P("cuts"))
    return jax.shard_map(
        per_device,
        mesh=mesh,
        in_specs=placed,
        out_specs=(P("grid", "cuts"), P("grid")),
        check_vma=False,
    )
```

time: 199 us -> 48.5 us (0.24)
  waiting for transfers between devices: 73.8 us -> 0 us
  other arithmetic: 62.8 us -> 0.63 us
  Pallas kernels: 0 us -> 40.1 us
  local copies, waits for them, and re-layouts: 20.5 us -> 5.44 us
  between operations: 16.1 us -> 1.31 us
  blocking collectives: 10.1 us -> 0 us
  matrix products: 8.85 us -> 0.78 us
  starting transfers between devices: 6.05 us -> 0 us
    psum x1 -> x0, waiting for transfers between devices: 72.9 us -> none  [per_device(): summed = lax.psum(partial_sums, 'grid')]
    another operation x9 -> x0, other arithmetic: 57.7 us -> none  [the longest x6 36.6 us: per_device(): factor = jnp.linalg.cholesky(intersection)]
    pallas_call x0 -> x1, Pallas kernels: none -> 40.1 us  [per_device(): pl.pallas_call(functools.partial(kernel, groups, slices), out_shape=(jax....]
    psum x1 -> x0, blocking collectives: 10.1 us -> none  [per_device(): density = core_density + lax.psum(contribution, 'cuts')]
    concatenate x1 -> x0, local copies, waits for them, and re-layouts: 9.22 us -> none  [with_halo(): x = jnp.concatenate([before, x, after], axis=dim)]
    ppermute x2 -> x0, starting transfers between devices: 6.02 us -> none  [the longest x1 3.08 us: with_halo(): after = lax.ppermute(leading, axis, down)]
    another operation x9 -> x0, local copies, waits for them, and re-layouts: 5.9 us -> none
    dot_general x4 -> x0, matrix products: 3.51 us -> none  [the longest x1 2.09 us: per_device(): lax.dot_general(orbitals, stacked, contract, preferred_element_type=jnp.f...]
  transfers between devices with their start and end apart: 3 -> 0, of which waited for: 2 -> 0; matrix products, arithmetic and copies ran while one was open for 1% -> 0% of each run, Pallas kernels for 0% -> 0%
where the time goes in v1:
time: 48.5 us; the launch traced here: 48.3 us
  Pallas kernels  40.1 us (83%)
  local copies, waits for them, and re-layouts  5.44 us (11%)
  between operations  1.31 us (3%)
  matrix products  0.78 us (2%)
  other arithmetic  0.63 us (1%)
    pallas_call x1, Pallas kernels, per_device(): pl.pallas_call(functools.partial(kernel, groups, slices), out_shape=(jax....  40.1 us
    unnamed x9, local copies, waits for them, and re-layouts  5.44 us

profile of v1, /device:TPU:0, one launch (start us, length us, event | category | flops | bytes accessed | tf_op | source)
XLA Modules:
  0.0 48.3 jit_solution(15264158747393785178)
XLA Ops:
  1.3 0.0 copy-start
  1.3 1.6 %copy-done = bf16[4096,256]{1,0:T(8,128)(2,1)S(1)} copy-done((bf16[4096,256]{1,0:T(8,128)(2,1)S(1)}, bf16[4096,256]{1,0:T(8,128)(2,1)}, u32[]{:S(2)}) %copy-start) | copy-done | bytes 2097176
  2.9 0.0 copy-start.1
  2.9 0.7 %copy-done.1 = f32[4096]{0:T(1024)S(1)} copy-done((f32[4096]{0:T(1024)S(1)}, f32[4096]{0:T(1024)}, u32[]{:S(2)}) %copy-start.1) | copy-done | bytes 16408
  3.6 0.0 copy-start.2
  3.6 0.7 %copy-done.2 = s32[256]{0:T(256)S(1)} copy-done((s32[256]{0:T(256)S(1)}, s32[256]{0:T(256)}, u32[]{:S(2)}) %copy-start.2) | copy-done | bytes 1048
  4.3 0.0 copy-start.3
  4.3 40.1 %shard_map.68 = (bf16[256,256]{1,0:T(8,128)(2,1)S(1)}, f32[32,128]{1,0:T(8,128)S(1)}) custom-call(bf16[4096,256]{1,0:T(8,128)(2,1)S(1)} %copy-done, f32[32,128]{1,0:T(8,128)S(1)} %bitcast.14, s32[1,256]{1,0:T(1,128)S(1)} %bitcast.15, s32[1]{0:T(128)S(6)} %copy.8.count_ref), custom_call_target="tpu_custom_call" | custom-call | flops 2147483648 | bytes 2097152 | tf_op jit(solution)/shard_map/pallas_call | solution.py:296
  44.4 0.0 copy-done.3
  44.4 0.6 %fusion.3 = f32[4096]{0:T(1024)} fusion(f32[4096]{0:T(1024)S(1)} %copy-done.3, f32[32,128]{1,0:T(8,128)S(1)} %get-tuple-element.5, f32[4096]{0:T(1024)S(1)} %copy-done.1), kind=kLoop, calls=%fused_computation.5 | loop fusion | flops 16384 | bytes 65536 | tf_op jit(solution)/shard_map/add | solution.py:339
  45.0 0.8 %fusion = bf16[4096,256]{0,1:T(8,128)(2,1)S(1)} fusion(bf16[256,256]{1,0:T(8,128)(2,1)S(1)} %get-tuple-element.4, bf16[4096,256]{1,0:T(8,128)(2,1)S(1)} %copy-done), kind=kOutput, calls=%fused_computation.1 | convolution fusion | flops 537919488 | bytes 4325376 | tf_op jit(solution)/shard_map/dot_general | solution.py:336
  45.8 2.5 %copy.7 = bf16[4096,256]{1,0:T(8,128)(2,1)} copy(bf16[4096,256]{0,1:T(8,128)(2,1)S(1)} %fusion) | data formatting | bytes 4194304
Async XLA Ops:
  1.3 1.6 %copy-start = (bf16[4096,256]{1,0:T(8,128)(2,1)S(1)}, bf16[4096,256]{1,0:T(8,128)(2,1)}, u32[]{:S(2)}) copy-start(bf16[4096,256]{1,0:T(8,128)(2,1)} %psi_hbm.1) | copy-start | bytes 6291460
  2.9 0.7 %copy-start.1 = (f32[4096]{0:T(1024)S(1)}, f32[4096]{0:T(1024)}, u32[]{:S(2)}) copy-start(f32[4096]{0:T(1024)} %param.6) | copy-start | bytes 49156
  3.6 0.7 %copy-start.2 = (s32[256]{0:T(256)S(1)}, s32[256]{0:T(256)}, u32[]{:S(2)}) copy-start(s32[256]{0:T(256)} %param.8) | copy-start | bytes 3076
  4.3 40.1 %copy-start.3 = (f32[4096]{0:T(1024)S(1)}, f32[4096]{0:T(1024)}, u32[]{:S(2)}) copy-start(f32[4096]{0:T(1024)} %param.7) | copy-start | bytes 49156

commit v2 on v1

--- a/solution.py
+++ b/solution.py
@@ -1,4 +1,5 @@
 import functools
+import math
 
 import jax
 import jax.numpy as jnp
@@ -26,44 +27,76 @@
     return high, middle, low
 
 
-def eliminate(left, right):
-    size = left.shape[0]
-    rows = lax.broadcasted_iota(jnp.int32, (size, lanes), 0)
-    tiles = [left[:, i : i + lanes] for i in range(0, left.shape[1], lanes)]
-    tiles += [right[:, i : i + lanes] for i in range(0, right.shape[1], lanes)]
-    for first in range(0, size, panel):
-        spread = [
-            jnp.broadcast_to(tiles[0][:, c : c + 1], (size, lanes))
-            for c in range(first, first + panel)
-        ]
-        for step in range(panel):
-            j = first + step
-            column = spread[step]
-            factor = column * (1.0 / column[j : j + 1, :])
-            factor = jnp.where(rows > j, factor, 0.0)
-            for c in range(step + 1, panel):
-                spread[c] = spread[c] - factor * spread[c][j : j + 1, :]
-            tiles = [t - factor * t[j : j + 1, :] for t in tiles]
-    at = lax.broadcasted_iota(jnp.int32, (size, lanes), 1)
-    pivots = jnp.sum(jnp.where(rows == at, tiles[0], 0.0), axis=1, keepdims=True)
-    scale = lax.rsqrt(pivots)
-    scale = scale * (1.5 - 0.5 * pivots * scale * scale)
-    tiles = [t * scale for t in tiles]
-    half = left.shape[1] // lanes
-    return jnp.concatenate(tiles[:half], axis=1), jnp.concatenate(tiles[half:], axis=1)
+def spread_rows(tile, r):
+    return jnp.broadcast_to(tile[r : r + 1, :], tile.shape)
+
+
+def eliminate(rows):
+    size, width = rows.shape
+    shape = (panel, lanes)
+    sub = lax.broadcasted_iota(jnp.int32, shape, 0)
+    at = lax.broadcasted_iota(jnp.int32, shape, 1)
+    count = size // panel
+    tiles = []
+    for g in range(count):
+        group = rows[g * panel : (g + 1) * panel]
+        tiles.append([group[:, i : i + lanes] for i in range(0, width, lanes)])
+        tiles[g].append((at == sub + g * panel).astype(jnp.float32))
+    done = []
+    for p in range(count):
+        below = range(p + 1, count)
+        spread = {
+            (g, c): jnp.broadcast_to(tiles[g][0][:, p * panel + c : p * panel + c + 1], shape)
+            for g in range(p, count)
+            for c in range(panel)
+        }
+        pivot = {(r, c): spread_rows(spread[p, c], r) for r in range(panel) for c in range(r + 1)}
+        lines = [[spread_rows(t, r) for t in tiles[p]] for r in range(panel)]
+        factors = {}
+        for j in range(panel):
+            inverse = 1.0 / pivot[j, j]
+            for r in range(j + 1, panel):
+                ratio = pivot[r, j] * inverse
+                for c in range(j + 1, r + 1):
+                    pivot[r, c] = pivot[r, c] - ratio * pivot[c, j]
+                lines[r] = [x - ratio * y for x, y in zip(lines[r], lines[j])]
+            for g in below:
+                factors[g, j] = spread[g, j] * inverse
+                for c in range(j + 1, panel):
+                    spread[g, c] = spread[g, c] - factors[g, j] * pivot[c, j]
+        for g in below:
+            for t in range(len(tiles[g])):
+                terms = [factors[g, j] * lines[j][t] for j in range(panel)]
+                while len(terms) > 1:
+                    terms = [x + y for x, y in zip(terms[::2], terms[1::2])]
+                tiles[g][t] = tiles[g][t] - terms[0]
+        scaled = []
+        for r in range(panel):
+            root = lax.rsqrt(pivot[r, r])
+            root = root * (1.5 - 0.5 * (pivot[r, r] * root) * root)
+            scaled.append([x * root for x in lines[r]])
+        merged = scaled[0]
+        for r in range(1, panel):
+            merged = [jnp.where(sub == r, x, y) for x, y in zip(scaled[r], merged)]
+        done.append(merged)
+    stack = [jnp.concatenate([group[t] for group in done], axis=0) for t in range(len(done[0]))]
+    return jnp.concatenate(stack[:-1], axis=1), stack[-1]
 
 
 def kernel(
     groups,
     slices,
     psi_hbm,
-    potential_ref,
-    occupation_ref,
+    potential_hbm,
+    occupation_hbm,
     count_ref,
     rotation_ref,
     density_ref,
     psi,
+    potential_ref,
+    occupation_ref,
     applied,
+    full,
     gram,
     landed,
     summed,
@@ -72,6 +105,7 @@
     mine,
     shares,
     load_sem,
+    small_sem,
     halo_send,
     halo_recv,
     scatter_send,
@@ -84,12 +118,21 @@
     points, width = psi_hbm.shape
     me = lax.axis_index("grid")
     cut = lax.axis_index("cuts")
-    part = width // groups
+    corner = width // 2
+    small_split = width % (2 * lanes) == 0 and (3 * width // 4) % (8 * groups) == 0
+    packed = 3 * width // 4 if small_split else width
+    parts = (packed // groups, width // groups)
     chunk = lanes * 8
     total_points = points * groups
 
     load = pltpu.make_async_copy(psi_hbm, psi.at[pl.ds(halo, points)], load_sem)
     load.start()
+    small = [
+        pltpu.make_async_copy(potential_hbm, potential_ref, small_sem.at[0]),
+        pltpu.make_async_copy(occupation_hbm, occupation_ref, small_sem.at[1]),
+    ]
+    for copy in small:
+        copy.start()
     barrier = pltpu.get_barrier_semaphore()
     for d in range(1, groups):
         pl.semaphore_signal(
@@ -101,15 +144,21 @@
         )
     load.wait()
 
-    gram[0] = jnp.zeros((width, width), jnp.float32)
+    full[...] = jnp.zeros((width, width), jnp.float32)
     gram[1] = jnp.zeros((width, width), jnp.float32)
 
     def overlap(i, carry):
         x = psi[pl.ds(pl.multiple_of(i * chunk, chunk) + halo, chunk), :]
-        gram[0] += lax.dot_general(x, x, columns, preferred_element_type=jnp.float32)
+        full[...] += lax.dot_general(x, x, columns, preferred_element_type=jnp.float32)
         return carry
 
     lax.fori_loop(0, points // chunk, overlap, 0)
+    if small_split:
+        gram[0, :corner, :] = full[:corner, :]
+        gram[0, corner:packed, :corner] = full[corner:packed, corner:]
+        gram[0, corner:packed, corner:] = full[packed:, corner:]
+    else:
+        gram[0] = full[...]
     pl.semaphore_wait(barrier, groups + slices - 2)
 
     up = pltpu.make_async_remote_copy(
@@ -131,16 +180,15 @@
     up.start()
     down.start()
 
-    own = pl.ds(pl.multiple_of(me * part, part), part)
-
     def scatter(which):
+        part = parts[which]
         copies = []
         for d in range(1, groups):
             to = lax.rem(me + d, groups)
             copies.append(
                 pltpu.make_async_remote_copy(
                     src_ref=gram.at[which, pl.ds(pl.multiple_of(to * part, part), part)],
-                    dst_ref=landed.at[which, d - 1],
+                    dst_ref=landed.at[which, d - 1, pl.ds(0, part)],
                     send_sem=scatter_send.at[which, d - 1],
                     recv_sem=scatter_recv.at[which, d - 1],
                     device_id={"grid": to},
@@ -152,11 +200,13 @@
         return copies
 
     def gather(which, copies):
+        part = parts[which]
+        own = pl.ds(pl.multiple_of(me * part, part), part)
         for copy in copies:
             copy.wait()
         total = gram[which, own, :]
         for d in range(groups - 1):
-            total = total + landed[which, d]
+            total = total + landed[which, d, :part, :]
         summed[which, own, :] = total * (1.0 / total_points)
         copies = []
         for d in range(1, groups):
@@ -177,6 +227,8 @@
     first = scatter(0)
     up.wait()
     down.wait()
+    for copy in small:
+        copy.wait()
 
     def ritz(i, carry):
         base = pl.multiple_of(i * chunk, chunk)
@@ -203,25 +255,29 @@
     identity = (row == column).astype(jnp.float32)
     for copy in first:
         copy.wait()
-    work[:, :width] = summed[0]
-    work[:, width:] = identity
+    if small_split:
+        work[:corner, :] = summed[0, :corner, :]
+        work[corner:, :corner] = jnp.zeros((width - corner, corner), jnp.float32)
+        work[corner:packed, corner:] = summed[0, corner:packed, :corner]
+        work[packed:, corner:] = summed[0, corner:packed, corner:]
+    else:
+        work[...] = summed[0]
 
     def factor(k, carry):
         here = pl.ds(pl.multiple_of(k * block, block), block)
-        back = lax.rem(width - k * block, width)
-        left = pltpu.roll(work[here, :width], back, 1)
-        left, right = eliminate(left, work[here, width:])
-        inverse_ref[here, :] = right
-        left = pltpu.roll(left, k * block, 1)
+        rows, own_inverse = eliminate(pltpu.roll(work[here, :], lax.rem(width - k * block, width), 1))
         at = lax.broadcasted_iota(jnp.int32, (block, width), 1)
-        left = jnp.where(at >= (k + 1) * block, left, 0.0)
-        lh, lm, ll = three_parts(left)
-        rh, rm, rl = three_parts(right)
-        lhs = jnp.concatenate([lh, lh, lm, lh, ll, lm], axis=0)
-        a = jnp.concatenate([lh, lm, lh, ll, lh, lm], axis=0)
-        b = jnp.concatenate([rh, rm, rh, rl, rh, rm], axis=0)
-        rhs = jnp.concatenate([a, b], axis=1)
-        work[...] -= lax.dot_general(lhs, rhs, columns, preferred_element_type=jnp.float32)
+        wide = jnp.concatenate([own_inverse] * (width // lanes), axis=1)
+        solved = pltpu.roll(jnp.where(at < block, wide, rows), k * block, 1)
+        ahead = jnp.where(at >= (k + 1) * block, solved, 0.0)
+        inverse_ref[here, :] = jnp.where(at >= (k + 1) * block, 0.0, solved)
+        ah, am, al = three_parts(ahead)
+        sh, sm, sl = three_parts(solved)
+        lhs = jnp.concatenate([ah, ah, am, ah, al, am], axis=0)
+        rhs = jnp.concatenate([sh, sm, sh, sl, sh, sm], axis=0)
+        update = lax.dot_general(lhs, rhs, columns, preferred_element_type=jnp.float32)
+        kept = (column < k * block) | (column >= (k + 1) * block)
+        work[...] = jnp.where(kept, work[...], 0.0) - update
         return carry
 
     blocks = width // block
@@ -286,8 +342,15 @@
     density_ref[...] = total
 
 
+def finish(psi_ref, rotation_ref, contribution_ref, core_ref, potential_ref, out_ref, mixed_ref):
+    coefficient = (3.0 / math.pi) ** (1.0 / 3.0)
+    rotated = jnp.dot(psi_ref[...], rotation_ref[...], preferred_element_type=jnp.float32)
+    out_ref[...] = rotated.astype(jnp.bfloat16)
+    root = jnp.exp(jnp.log(core_ref[...] + contribution_ref[...]) * (1.0 / 3.0))
+    mixed_ref[...] = (1.0 - mixing) * potential_ref[...] + mixing * (-coefficient * root)
+
+
 def per_device(orbitals, potential, core_density, occupation, slice_counts):
-    coefficient = (3.0 / jnp.pi) ** (1.0 / 3.0)
     points, width = orbitals.shape
     groups, slices = (lax.axis_size("grid"), lax.axis_size("cuts"))
     folded = (points // lanes, lanes)
@@ -300,23 +363,27 @@
             jax.ShapeDtypeStruct(folded, jnp.float32),
         ),
         in_specs=[
-            pl.BlockSpec(memory_space=pl.ANY),
-            vmem,
-            vmem,
+            pl.BlockSpec(memory_space=pltpu.HBM),
+            pl.BlockSpec(memory_space=pltpu.HBM),
+            pl.BlockSpec(memory_space=pltpu.HBM),
             pl.BlockSpec(memory_space=pltpu.SMEM),
         ],
         out_specs=(vmem, vmem),
         scratch_shapes=[
             pltpu.VMEM((points + 2 * halo, width), jnp.bfloat16),
+            pltpu.VMEM(folded, jnp.float32),
+            pltpu.VMEM((1, width), jnp.int32),
             pltpu.VMEM((8 * lanes, width), jnp.bfloat16),
+            pltpu.VMEM((width, width), jnp.float32),
             pltpu.VMEM((2, width, width), jnp.float32),
             pltpu.VMEM((2, groups - 1, part, width), jnp.float32),
             pltpu.VMEM((2, width, width), jnp.float32),
-            pltpu.VMEM((width, 2 * width), jnp.float32),
+            pltpu.VMEM((width, width), jnp.float32),
             pltpu.VMEM((width, width), jnp.float32),
             pltpu.VMEM(folded, jnp.float32),
             pltpu.VMEM((slices,) + folded, jnp.float32),
             pltpu.SemaphoreType.DMA,
+            pltpu.SemaphoreType.DMA((2,)),
             pltpu.SemaphoreType.DMA((2,)),
             pltpu.SemaphoreType.DMA((2,)),
             pltpu.SemaphoreType.DMA((2, groups - 1)),
@@ -333,11 +400,23 @@
             flops=8 * points * width * width, bytes_accessed=2 * points * width, transcendentals=0
         ),
     )(orbitals, potential.reshape(folded), occupation.reshape(1, width), slice_counts)
-    rotated = jnp.dot(orbitals, rotation, preferred_element_type=jnp.float32)
-    orbitals_out = rotated.astype(jnp.bfloat16)
-    density = core_density + contribution.reshape(points)
-    potential_out = (1.0 - mixing) * potential + mixing * (-coefficient * jnp.cbrt(density))
-    return (orbitals_out, potential_out)
+    chunk = 8 * lanes
+    tall = pl.BlockSpec((chunk, width), lambda i: (i, 0))
+    flat = pl.BlockSpec((8, lanes), lambda i: (i, 0))
+    orbitals_out, potential_out = pl.pallas_call(
+        finish,
+        grid=(points // chunk,),
+        out_shape=(
+            jax.ShapeDtypeStruct((points, width), jnp.bfloat16),
+            jax.ShapeDtypeStruct(folded, jnp.float32),
+        ),
+        in_specs=[tall, pl.BlockSpec((width, width), lambda i: (0, 0)), flat, flat, flat],
+        out_specs=(tall, flat),
+        cost_estimate=pl.CostEstimate(
+            flops=2 * points * width * width, bytes_accessed=4 * points * width, transcendentals=0
+        ),
+    )(orbitals, rotation, contribution, core_density.reshape(folded), potential.reshape(folded))
+    return (orbitals_out, potential_out.reshape(points))
 
 
 def solution(mesh):

time: 48.5 us -> 47.9 us (0.988)
  Pallas kernels: 40.1 us -> 42.1 us
  local copies, waits for them, and re-layouts: 5.44 us -> 4.22 us
  matrix products: 0.78 us -> 0 us
  other arithmetic: 0.63 us -> 0 us
    pallas_call x0 -> x1, Pallas kernels: none -> 4.38 us  [per_device(): pl.pallas_call(finish, grid=(points // chunk,), out_shape=(jax.ShapeDtype...]
    pallas_call x1, Pallas kernels: 40.1 us -> 37.7 us  [per_device(): pl.pallas_call(functools.partial(kernel, groups, slices), out_shape=(jax....]
    unnamed x9 -> x10, local copies, waits for them, and re-layouts: 5.44 us -> 4.22 us
    dot_general x1 -> x0, matrix products: 0.78 us -> none  [per_device(): rotated = jnp.dot(orbitals, rotation, preferred_element_type=jnp.float32)]
    add x1 -> x0, other arithmetic: 0.63 us -> none  [per_device(): (1.0 - mixing) * potential + mixing * (-coefficient * jnp.cbrt(density))]
where the time goes in v2:
time: 47.9 us; the launch traced here: 47.6 us
  Pallas kernels  42.1 us (88%)
  local copies, waits for them, and re-layouts  4.22 us (9%)
  between operations  1.3 us (3%)
    pallas_call x1, Pallas kernels, per_device(): pl.pallas_call(functools.partial(kernel, groups, slices), out_shape=(jax....  37.7 us
    pallas_call x1, Pallas kernels, per_device(): pl.pallas_call(finish, grid=(points // chunk,), out_shape=(jax.ShapeDtype...  4.38 us
    unnamed x10, local copies, waits for them, and re-layouts  4.22 us

profile of v2, /device:TPU:0, one launch (start us, length us, event | category | flops | bytes accessed | tf_op | source)
XLA Modules:
  0.0 47.6 jit_solution(15577678468390179765)
XLA Ops:
  1.3 0.0 copy-start
  1.3 1.6 %copy-done = bf16[4096,256]{1,0:T(8,128)(2,1)S(1)} copy-done((bf16[4096,256]{1,0:T(8,128)(2,1)S(1)}, bf16[4096,256]{1,0:T(8,128)(2,1)}, u32[]{:S(2)}) %copy-start) | copy-done | bytes 2097176
  2.9 0.0 copy-start.2
  2.9 0.7 %copy-done.2 = f32[4096]{0:T(1024)S(1)} copy-done((f32[4096]{0:T(1024)S(1)}, f32[4096]{0:T(1024)}, u32[]{:S(2)}) %copy-start.2) | copy-done | bytes 16408
  3.6 0.0 copy-start.4
  3.6 0.7 %copy-done.4 = s32[256]{0:T(256)S(1)} copy-done((s32[256]{0:T(256)S(1)}, s32[256]{0:T(256)}, u32[]{:S(2)}) %copy-start.4) | copy-done | bytes 1048
  4.3 37.7 %shard_map.68 = (bf16[256,256]{1,0:T(8,128)(2,1)S(1)}, f32[32,128]{1,0:T(8,128)S(1)}) custom-call(bf16[4096,256]{1,0:T(8,128)(2,1)S(1)} %copy-done, f32[32,128]{1,0:T(8,128)S(1)} %bitcast.5, s32[1,256]{1,0:T(1,128)S(1)} %bitcast.6, s32[1]{0:T(128)S(6)} %copy.7.count_ref), custom_call_target="tpu_custom_call" | custom-call | flops 2147483648 | bytes 2097152 | tf_op jit(solution)/shard_map/pallas_call | solution.py:359
  42.0 0.0 copy-start.1
  42.0 0.6 %copy-done.1 = bf16[256,256]{1,0:T(8,128)(2,1)} copy-done((bf16[256,256]{1,0:T(8,128)(2,1)}, bf16[256,256]{1,0:T(8,128)(2,1)S(1)}, u32[]{:S(2)}) %copy-start.1) | copy-done | bytes 131096
  42.6 0.0 copy-start.3
  42.6 0.6 %copy-done.3 = f32[32,128]{1,0:T(8,128)} copy-done((f32[32,128]{1,0:T(8,128)}, f32[32,128]{1,0:T(8,128)S(1)}, u32[]{:S(2)}) %copy-start.3) | copy-done | bytes 16408
  43.2 4.4 %shard_map.69 = (bf16[4096,256]{1,0:T(8,128)(2,1)}, f32[32,128]{1,0:T(8,128)}) custom-call(bf16[4096,256]{1,0:T(8,128)(2,1)} %psi_ref.1, bf16[256,256]{1,0:T(8,128)(2,1)} %copy-done.1, f32[32,128]{1,0:T(8,128)} %copy-done.3, f32[32,128]{1,0:T(8,128)} %bitcast.7, f32[32,128]{1,0:T(8,128)} %bitcast.4), custom_call_target="tpu_custom_call" | custom-call | flops 536870912 | bytes 4194304 | tf_op jit(solution)/shard_map/pallas_call | solution.py:406
Async XLA Ops:
  1.3 1.6 %copy-start = (bf16[4096,256]{1,0:T(8,128)(2,1)S(1)}, bf16[4096,256]{1,0:T(8,128)(2,1)}, u32[]{:S(2)}) copy-start(bf16[4096,256]{1,0:T(8,128)(2,1)} %psi_ref.1) | copy-start | bytes 6291460
  2.9 0.7 %copy-start.2 = (f32[4096]{0:T(1024)S(1)}, f32[4096]{0:T(1024)}, u32[]{:S(2)}) copy-start(f32[4096]{0:T(1024)} %param.6) | copy-start | bytes 49156
  3.6 0.7 %copy-start.4 = (s32[256]{0:T(256)S(1)}, s32[256]{0:T(256)}, u32[]{:S(2)}) copy-start(s32[256]{0:T(256)} %param.8) | copy-start | bytes 3076
  42.0 0.6 %copy-start.1 = (bf16[256,256]{1,0:T(8,128)(2,1)}, bf16[256,256]{1,0:T(8,128)(2,1)S(1)}, u32[]{:S(2)}) copy-start(bf16[256,256]{1,0:T(8,128)(2,1)S(1)} %get-tuple-element.6.rotation_ref) | copy-start | bytes 393220
  42.6 0.6 %copy-start.3 = (f32[32,128]{1,0:T(8,128)}, f32[32,128]{1,0:T(8,128)S(1)}, u32[]{:S(2)}) copy-start(f32[32,128]{1,0:T(8,128)S(1)} %get-tuple-element.7.contribution_ref) | copy-start | bytes 49156

commit v3 on v2

--- a/solution.py
+++ b/solution.py
@@ -54,11 +54,11 @@
         lines = [[spread_rows(t, r) for t in tiles[p]] for r in range(panel)]
         factors = {}
         for j in range(panel):
-            inverse = 1.0 / pivot[j, j]
+            inverse = pltpu.reciprocal(pivot[j, j], approx=True)
             for r in range(j + 1, panel):
                 ratio = pivot[r, j] * inverse
                 for c in range(j + 1, r + 1):
-                    pivot[r, c] = pivot[r, c] - ratio * pivot[c, j]
+                    pivot[r, c] = pivot[r, c] - (pivot[r, j] * pivot[c, j]) * inverse
                 lines[r] = [x - ratio * y for x, y in zip(lines[r], lines[j])]
             for g in below:
                 factors[g, j] = spread[g, j] * inverse
@@ -73,7 +73,6 @@
         scaled = []
         for r in range(panel):
             root = lax.rsqrt(pivot[r, r])
-            root = root * (1.5 - 0.5 * (pivot[r, r] * root) * root)
             scaled.append([x * root for x in lines[r]])
         merged = scaled[0]
         for r in range(1, panel):
@@ -88,13 +87,16 @@
     slices,
     psi_hbm,
     potential_hbm,
+    core_hbm,
     occupation_hbm,
     count_ref,
-    rotation_ref,
-    density_ref,
+    out_hbm,
+    mixed_ref,
     psi,
     potential_ref,
+    core_ref,
     occupation_ref,
+    out,
     applied,
     full,
     gram,
@@ -106,6 +108,7 @@
     shares,
     load_sem,
     small_sem,
+    store_sem,
     halo_send,
     halo_recv,
     scatter_send,
@@ -125,11 +128,19 @@
     chunk = lanes * 8
     total_points = points * groups
 
-    load = pltpu.make_async_copy(psi_hbm, psi.at[pl.ds(halo, points)], load_sem)
-    load.start()
+    steps = points // chunk
+    loads = [
+        pltpu.make_async_copy(
+            psi_hbm.at[pl.ds(i * chunk, chunk)], psi.at[pl.ds(halo + i * chunk, chunk)], load_sem.at[i]
+        )
+        for i in range(steps)
+    ]
+    for copy in loads:
+        copy.start()
     small = [
         pltpu.make_async_copy(potential_hbm, potential_ref, small_sem.at[0]),
         pltpu.make_async_copy(occupation_hbm, occupation_ref, small_sem.at[1]),
+        pltpu.make_async_copy(core_hbm, core_ref, small_sem.at[2]),
     ]
     for copy in small:
         copy.start()
@@ -142,17 +153,13 @@
         pl.semaphore_signal(
             barrier, inc=1, device_id={"cuts": lax.rem(cut + d, slices)}, device_id_type=pl.DeviceIdType.MESH
         )
-    load.wait()
-
     full[...] = jnp.zeros((width, width), jnp.float32)
     gram[1] = jnp.zeros((width, width), jnp.float32)
 
-    def overlap(i, carry):
-        x = psi[pl.ds(pl.multiple_of(i * chunk, chunk) + halo, chunk), :]
+    for i in range(steps):
+        loads[i].wait()
+        x = psi[pl.ds(halo + i * chunk, chunk), :]
         full[...] += lax.dot_general(x, x, columns, preferred_element_type=jnp.float32)
-        return carry
-
-    lax.fori_loop(0, points // chunk, overlap, 0)
     if small_split:
         gram[0, :corner, :] = full[:corner, :]
         gram[0, corner:packed, :corner] = full[corner:packed, corner:]
@@ -246,8 +253,9 @@
         gram[1] += lax.dot_general(x, applied[...], columns, preferred_element_type=jnp.float32)
         return carry
 
-    lax.fori_loop(0, points // chunk, ritz, 0)
+    lax.fori_loop(0, steps // 2, ritz, 0)
     first = gather(0, first)
+    lax.fori_loop(steps // 2, steps, ritz, 0)
     second = scatter(1)
 
     row = lax.broadcasted_iota(jnp.int32, (width, width), 0)
@@ -299,15 +307,19 @@
         precision=highest,
         preferred_element_type=jnp.float32,
     ).astype(jnp.bfloat16)
-    rotation_ref[...] = rotation
 
     state = lax.broadcasted_iota(jnp.int32, (1, width), 1)
     live = (state < count_ref[0]).astype(jnp.float32)
     weights = occupation_ref[...].astype(jnp.float32) * live / (2.0 * width * slices)
 
-    def contribute(i, carry):
-        x = psi[pl.ds(pl.multiple_of(i * chunk, chunk) + halo, chunk), :]
-        rotated = jnp.dot(x, rotation_ref[...], preferred_element_type=jnp.float32)
+    stores = []
+    for i in range(steps):
+        x = psi[pl.ds(halo + i * chunk, chunk), :]
+        rotated = jnp.dot(x, rotation, preferred_element_type=jnp.float32)
+        out[pl.ds(i * chunk, chunk), :] = rotated.astype(jnp.bfloat16)
+        here = pl.ds(i * chunk, chunk)
+        stores.append(pltpu.make_async_copy(out.at[here], out_hbm.at[here], store_sem.at[i]))
+        stores[i].start()
         square = rotated * rotated * weights
         narrow = square[:, :lanes]
         for c in range(lanes, width, lanes):
@@ -315,10 +327,7 @@
         sums = [
             jnp.sum(narrow[s * lanes : (s + 1) * lanes].T, axis=0, keepdims=True) for s in range(8)
         ]
-        mine[pl.ds(pl.multiple_of(i * 8, 8), 8), :] = jnp.concatenate(sums, axis=0)
-        return carry
-
-    lax.fori_loop(0, points // chunk, contribute, 0)
+        mine[i * 8 : (i + 1) * 8, :] = jnp.concatenate(sums, axis=0)
     copies = []
     for d in range(1, slices):
         copies.append(
@@ -336,18 +345,14 @@
     shares[cut] = mine[...]
     for copy in copies:
         copy.wait()
-    total = shares[0]
-    for c in range(1, slices):
-        total = total + shares[c]
-    density_ref[...] = total
-
-
-def finish(psi_ref, rotation_ref, contribution_ref, core_ref, potential_ref, out_ref, mixed_ref):
+    density = core_ref[...]
+    for c in range(slices):
+        density = density + shares[c]
     coefficient = (3.0 / math.pi) ** (1.0 / 3.0)
-    rotated = jnp.dot(psi_ref[...], rotation_ref[...], preferred_element_type=jnp.float32)
-    out_ref[...] = rotated.astype(jnp.bfloat16)
-    root = jnp.exp(jnp.log(core_ref[...] + contribution_ref[...]) * (1.0 / 3.0))
+    root = jnp.exp(jnp.log(density) * (1.0 / 3.0))
     mixed_ref[...] = (1.0 - mixing) * potential_ref[...] + mixing * (-coefficient * root)
+    for copy in stores:
+        copy.wait()
 
 
 def per_device(orbitals, potential, core_density, occupation, slice_counts):
@@ -355,24 +360,22 @@
     groups, slices = (lax.axis_size("grid"), lax.axis_size("cuts"))
     folded = (points // lanes, lanes)
     part = width // groups
-    vmem = pl.BlockSpec(memory_space=pltpu.VMEM)
-    rotation, contribution = pl.pallas_call(
+    steps = points // (8 * lanes)
+    hbm = pl.BlockSpec(memory_space=pltpu.HBM)
+    orbitals_out, potential_out = pl.pallas_call(
         functools.partial(kernel, groups, slices),
         out_shape=(
-            jax.ShapeDtypeStruct((width, width), jnp.bfloat16),
+            jax.ShapeDtypeStruct((points, width), jnp.bfloat16),
             jax.ShapeDtypeStruct(folded, jnp.float32),
         ),
-        in_specs=[
-            pl.BlockSpec(memory_space=pltpu.HBM),
-            pl.BlockSpec(memory_space=pltpu.HBM),
-            pl.BlockSpec(memory_space=pltpu.HBM),
-            pl.BlockSpec(memory_space=pltpu.SMEM),
-        ],
-        out_specs=(vmem, vmem),
+        in_specs=[hbm, hbm, hbm, hbm, pl.BlockSpec(memory_space=pltpu.SMEM)],
+        out_specs=(hbm, pl.BlockSpec(memory_space=pltpu.VMEM)),
         scratch_shapes=[
             pltpu.VMEM((points + 2 * halo, width), jnp.bfloat16),
             pltpu.VMEM(folded, jnp.float32),
+            pltpu.VMEM(folded, jnp.float32),
             pltpu.VMEM((1, width), jnp.int32),
+            pltpu.VMEM((points, width), jnp.bfloat16),
             pltpu.VMEM((8 * lanes, width), jnp.bfloat16),
             pltpu.VMEM((width, width), jnp.float32),
             pltpu.VMEM((2, width, width), jnp.float32),
@@ -382,8 +385,9 @@
             pltpu.VMEM((width, width), jnp.float32),
             pltpu.VMEM(folded, jnp.float32),
             pltpu.VMEM((slices,) + folded, jnp.float32),
-            pltpu.SemaphoreType.DMA,
-            pltpu.SemaphoreType.DMA((2,)),
+            pltpu.SemaphoreType.DMA((steps,)),
+            pltpu.SemaphoreType.DMA((3,)),
+            pltpu.SemaphoreType.DMA((steps,)),
             pltpu.SemaphoreType.DMA((2,)),
             pltpu.SemaphoreType.DMA((2,)),
             pltpu.SemaphoreType.DMA((2, groups - 1)),
@@ -394,28 +398,18 @@
             pltpu.SemaphoreType.DMA((slices - 1,)),
         ],
         compiler_params=pltpu.CompilerParams(
-            collective_id=0, has_side_effects=True, vmem_limit_bytes=40 * 1024 * 1024
+            collective_id=0, has_side_effects=True, vmem_limit_bytes=60 * 1024 * 1024
         ),
         cost_estimate=pl.CostEstimate(
             flops=8 * points * width * width, bytes_accessed=2 * points * width, transcendentals=0
         ),
-    )(orbitals, potential.reshape(folded), occupation.reshape(1, width), slice_counts)
-    chunk = 8 * lanes
-    tall = pl.BlockSpec((chunk, width), lambda i: (i, 0))
-    flat = pl.BlockSpec((8, lanes), lambda i: (i, 0))
-    orbitals_out, potential_out = pl.pallas_call(
-        finish,
-        grid=(points // chunk,),
-        out_shape=(
-            jax.ShapeDtypeStruct((points, width), jnp.bfloat16),
-            jax.ShapeDtypeStruct(folded, jnp.float32),
-        ),
-        in_specs=[tall, pl.BlockSpec((width, width), lambda i: (0, 0)), flat, flat, flat],
-        out_specs=(tall, flat),
-        cost_estimate=pl.CostEstimate(
-            flops=2 * points * width * width, bytes_accessed=4 * points * width, transcendentals=0
-        ),
-    )(orbitals, rotation, contribution, core_density.reshape(folded), potential.reshape(folded))
+    )(
+        orbitals,
+        potential.reshape(folded),
+        core_density.reshape(folded),
+        occupation.reshape(1, width),
+        slice_counts,
+    )
     return (orbitals_out, potential_out.reshape(points))
 
 

time: 47.9 us -> 42.3 us (0.88)
  Pallas kernels: 42.1 us -> 37.2 us
  local copies, waits for them, and re-layouts: 4.22 us -> 3.66 us
    pallas_call x1 -> x0, Pallas kernels: 4.38 us -> none  [per_device(): pl.pallas_call(finish, grid=(points // chunk,), out_shape=(jax.ShapeDtype...]
    unnamed x10 -> x4, local copies, waits for them, and re-layouts: 4.22 us -> 3.66 us
    pallas_call x1, Pallas kernels: 37.7 us -> 37.2 us  [per_device(): pl.pallas_call(functools.partial(kernel, groups, slices), out_shape=(jax....]
where the time goes in v3:
time: 42.3 us; the launch traced here: 42.2 us
  Pallas kernels  37.2 us (88%)
  local copies, waits for them, and re-layouts  3.66 us (9%)
  between operations  1.29 us (3%)
    pallas_call x1, Pallas kernels, per_device(): pl.pallas_call(functools.partial(kernel, groups, slices), out_shape=(jax....  37.2 us
    unnamed x4, local copies, waits for them, and re-layouts  3.66 us

profile of v3, /device:TPU:0, one launch (start us, length us, event | category | flops | bytes accessed | tf_op | source)
XLA Modules:
  0.0 42.2 jit_solution(18033576424457576646)
XLA Ops:
  1.3 37.2 %shard_map.68 = (bf16[4096,256]{1,0:T(8,128)(2,1)}, f32[32,128]{1,0:T(8,128)}) custom-call(bf16[4096,256]{1,0:T(8,128)(2,1)} %psi_hbm.1, f32[32,128]{1,0:T(8,128)} %bitcast.5, f32[32,128]{1,0:T(8,128)} %bitcast.6, s32[1,256]{1,0:T(1,128)} %bitcast.7, s32[1]{0:T(128)S(6)} %copy.9.count_ref), custom_call_target="tpu_custom_call" | custom-call | flops 2147483648 | bytes 2097152 | tf_op jit(solution)/shard_map/pallas_call | solution.py:365
  38.5 0.0 copy-start
  38.5 3.0 %copy.10 = bf16[4096,256]{1,0:T(8,128)(2,1)} copy(bf16[4096,256]{1,0:T(8,128)(2,1)} %get-tuple-element.8) | data formatting | bytes 4194304
  41.5 0.0 copy-done
  41.5 0.6 %copy.11 = f32[4096]{0:T(1024)} copy(f32[4096]{0:T(1024)S(1)} %bitcast.4) | data formatting | bytes 32768
Async XLA Ops:
  38.5 3.1 %copy-start = (f32[32,128]{1,0:T(8,128)S(1)}, f32[32,128]{1,0:T(8,128)}, u32[]{:S(2)}) copy-start(f32[32,128]{1,0:T(8,128)} %get-tuple-element.5) | copy-start | bytes 49156

commit v4 on v3

--- a/solution.py
+++ b/solution.py
@@ -16,6 +16,7 @@
 panel = 8
 columns = (((0,), (0,)), ((), ()))
 across = (((1,), (1,)), ((), ()))
+along = (((1,), (0,)), ((), ()))
 highest = lax.Precision.HIGHEST
 
 
@@ -99,11 +100,10 @@
     out,
     applied,
     full,
-    gram,
+    partial,
     landed,
     summed,
-    work,
-    inverse_ref,
+    factors,
     mine,
     shares,
     load_sem,
@@ -121,10 +121,6 @@
     points, width = psi_hbm.shape
     me = lax.axis_index("grid")
     cut = lax.axis_index("cuts")
-    corner = width // 2
-    small_split = width % (2 * lanes) == 0 and (3 * width // 4) % (8 * groups) == 0
-    packed = 3 * width // 4 if small_split else width
-    parts = (packed // groups, width // groups)
     chunk = lanes * 8
     total_points = points * groups
 
@@ -154,18 +150,16 @@
             barrier, inc=1, device_id={"cuts": lax.rem(cut + d, slices)}, device_id_type=pl.DeviceIdType.MESH
         )
     full[...] = jnp.zeros((width, width), jnp.float32)
-    gram[1] = jnp.zeros((width, width), jnp.float32)
 
     for i in range(steps):
         loads[i].wait()
         x = psi[pl.ds(halo + i * chunk, chunk), :]
         full[...] += lax.dot_general(x, x, columns, preferred_element_type=jnp.float32)
-    if small_split:
-        gram[0, :corner, :] = full[:corner, :]
-        gram[0, corner:packed, :corner] = full[corner:packed, corner:]
-        gram[0, corner:packed, corner:] = full[packed:, corner:]
-    else:
-        gram[0] = full[...]
+    stages = (
+        lambda: full[:lanes, :lanes],
+        lambda: jnp.concatenate([full[:lanes, lanes:], full[lanes:, lanes:]], axis=0),
+        lambda: full[...],
+    )
     pl.semaphore_wait(barrier, groups + slices - 2)
 
     up = pltpu.make_async_remote_copy(
@@ -188,14 +182,17 @@
     down.start()
 
     def scatter(which):
-        part = parts[which]
+        values = stages[which]()
+        part = partial[which].shape[1]
+        for i in range(groups):
+            partial[which][i] = values[i * part : (i + 1) * part]
         copies = []
         for d in range(1, groups):
             to = lax.rem(me + d, groups)
             copies.append(
                 pltpu.make_async_remote_copy(
-                    src_ref=gram.at[which, pl.ds(pl.multiple_of(to * part, part), part)],
-                    dst_ref=landed.at[which, d - 1, pl.ds(0, part)],
+                    src_ref=partial[which].at[to],
+                    dst_ref=landed[which].at[d - 1],
                     send_sem=scatter_send.at[which, d - 1],
                     recv_sem=scatter_recv.at[which, d - 1],
                     device_id={"grid": to},
@@ -207,20 +204,18 @@
         return copies
 
     def gather(which, copies):
-        part = parts[which]
-        own = pl.ds(pl.multiple_of(me * part, part), part)
         for copy in copies:
             copy.wait()
-        total = gram[which, own, :]
+        total = partial[which][me]
         for d in range(groups - 1):
-            total = total + landed[which, d, :part, :]
-        summed[which, own, :] = total * (1.0 / total_points)
+            total = total + landed[which][d]
+        summed[which][me] = total * (1.0 / total_points)
         copies = []
         for d in range(1, groups):
             copies.append(
                 pltpu.make_async_remote_copy(
-                    src_ref=summed.at[which, own],
-                    dst_ref=summed.at[which, own],
+                    src_ref=summed[which].at[me],
+                    dst_ref=summed[which].at[me],
                     send_sem=gather_send.at[which, d - 1],
                     recv_sem=gather_recv.at[which, d - 1],
                     device_id={"grid": lax.rem(me + d, groups)},
@@ -231,7 +226,13 @@
             copy.start()
         return copies
 
+    def collect(which, copies):
+        for copy in copies:
+            copy.wait()
+        return jnp.concatenate([summed[which][i] for i in range(groups)], axis=0)
+
     first = scatter(0)
+    second = scatter(1)
     up.wait()
     down.wait()
     for copy in small:
@@ -250,63 +251,63 @@
             kinetic = -0.5 * (after + before - 2.0 * middle)
             applied[s * lanes : (s + 1) * lanes, :] = (kinetic + local * middle).astype(jnp.bfloat16)
         x = psi[pl.ds(base + halo, chunk), :]
-        gram[1] += lax.dot_general(x, applied[...], columns, preferred_element_type=jnp.float32)
+        full[...] += lax.dot_general(x, applied[...], columns, preferred_element_type=jnp.float32)
         return carry
 
-    lax.fori_loop(0, steps // 2, ritz, 0)
+    full[...] = jnp.zeros((width, width), jnp.float32)
+    lax.fori_loop(0, steps // 4, ritz, 0)
     first = gather(0, first)
+    lax.fori_loop(steps // 4, steps // 2, ritz, 0)
+    second = gather(1, second)
     lax.fori_loop(steps // 2, steps, ritz, 0)
-    second = scatter(1)
-
+    third = scatter(2)
+
+    at = lax.broadcasted_iota(jnp.int32, (block, lanes), 1)
+    column = lax.broadcasted_iota(jnp.int32, (lanes, lanes), 1)
+
+    def factorise(matrix, inverse_ref):
+        def factor(k, work):
+            rows, own = eliminate(work[:block])
+            solved = jnp.where(at < block, own, rows)
+            ahead = jnp.where((at >= block) & (at < lanes - k * block), solved, 0.0)
+            here = pl.ds(pl.multiple_of(k * block, block), block)
+            turned = pltpu.roll(solved, k * block, 1)
+            inverse_ref[here, :] = jnp.where(at >= (k + 1) * block, 0.0, turned)
+            ah, am, al = three_parts(ahead)
+            sh, sm, sl = three_parts(solved)
+            lhs = jnp.concatenate([ah, ah, am, ah, al, am], axis=0)
+            rhs = jnp.concatenate([sh, sm, sh, sl, sh, sm], axis=0)
+            update = lax.dot_general(lhs, rhs, columns, preferred_element_type=jnp.float32)
+            work = jnp.where(column < block, 0.0, work) - update
+            work = jnp.concatenate([work[block:], work[:block]], axis=0)
+            return pltpu.roll(work, lanes - block, 1)
+
+        lax.fori_loop(0, lanes // block, factor, matrix)
+        return inverse_ref[...]
+
+    def exact(x, y, contract):
+        return lax.dot_general(
+            x, y, contract, precision=highest, preferred_element_type=jnp.float32
+        )
+
+    lead = factorise(collect(0, first), factors.at[0])
+    rest = collect(1, second)
+    coupled = exact(lead, rest[:lanes], along)
+    third = gather(2, third)
+    tail = factorise(rest[lanes:] - exact(coupled, coupled, columns), factors.at[1])
+    corner = exact(tail, exact(coupled, lead, columns), along)
+    inverse = jnp.concatenate(
+        [
+            jnp.concatenate([lead, jnp.zeros((lanes, lanes), jnp.float32)], axis=1),
+            jnp.concatenate([-corner, tail], axis=1),
+        ],
+        axis=0,
+    )
+    ritz_sum = collect(2, third)
     row = lax.broadcasted_iota(jnp.int32, (width, width), 0)
-    column = lax.broadcasted_iota(jnp.int32, (width, width), 1)
-    identity = (row == column).astype(jnp.float32)
-    for copy in first:
-        copy.wait()
-    if small_split:
-        work[:corner, :] = summed[0, :corner, :]
-        work[corner:, :corner] = jnp.zeros((width - corner, corner), jnp.float32)
-        work[corner:packed, corner:] = summed[0, corner:packed, :corner]
-        work[packed:, corner:] = summed[0, corner:packed, corner:]
-    else:
-        work[...] = summed[0]
-
-    def factor(k, carry):
-        here = pl.ds(pl.multiple_of(k * block, block), block)
-        rows, own_inverse = eliminate(pltpu.roll(work[here, :], lax.rem(width - k * block, width), 1))
-        at = lax.broadcasted_iota(jnp.int32, (block, width), 1)
-        wide = jnp.concatenate([own_inverse] * (width // lanes), axis=1)
-        solved = pltpu.roll(jnp.where(at < block, wide, rows), k * block, 1)
-        ahead = jnp.where(at >= (k + 1) * block, solved, 0.0)
-        inverse_ref[here, :] = jnp.where(at >= (k + 1) * block, 0.0, solved)
-        ah, am, al = three_parts(ahead)
-        sh, sm, sl = three_parts(solved)
-        lhs = jnp.concatenate([ah, ah, am, ah, al, am], axis=0)
-        rhs = jnp.concatenate([sh, sm, sh, sl, sh, sm], axis=0)
-        update = lax.dot_general(lhs, rhs, columns, preferred_element_type=jnp.float32)
-        kept = (column < k * block) | (column >= (k + 1) * block)
-        work[...] = jnp.where(kept, work[...], 0.0) - update
-        return carry
-
-    blocks = width // block
-    lax.fori_loop(0, blocks // 2, factor, 0)
-    second = gather(1, second)
-    lax.fori_loop(blocks // 2, blocks, factor, 0)
-    for copy in second:
-        copy.wait()
-
-    inverse = inverse_ref[...]
-    projected = jnp.dot(inverse, summed[1], precision=highest, preferred_element_type=jnp.float32)
-    projected = lax.dot_general(
-        projected, inverse, across, precision=highest, preferred_element_type=jnp.float32
-    )
-    rotation = lax.dot_general(
-        inverse,
-        identity - step_size * projected,
-        columns,
-        precision=highest,
-        preferred_element_type=jnp.float32,
-    ).astype(jnp.bfloat16)
+    identity = (row == lax.broadcasted_iota(jnp.int32, (width, width), 1)).astype(jnp.float32)
+    projected = exact(exact(inverse, ritz_sum, along), inverse, across)
+    rotation = exact(inverse, identity - step_size * projected, columns).astype(jnp.bfloat16)
 
     state = lax.broadcasted_iota(jnp.int32, (1, width), 1)
     live = (state < count_ref[0]).astype(jnp.float32)
@@ -359,7 +360,12 @@
     points, width = orbitals.shape
     groups, slices = (lax.axis_size("grid"), lax.axis_size("cuts"))
     folded = (points // lanes, lanes)
-    part = width // groups
+    assert width == 2 * lanes
+    parts = [
+        (lanes // groups, lanes),
+        (width // groups, lanes),
+        (width // groups, width),
+    ]
     steps = points // (8 * lanes)
     hbm = pl.BlockSpec(memory_space=pltpu.HBM)
     orbitals_out, potential_out = pl.pallas_call(
@@ -378,11 +384,10 @@
             pltpu.VMEM((points, width), jnp.bfloat16),
             pltpu.VMEM((8 * lanes, width), jnp.bfloat16),
             pltpu.VMEM((width, width), jnp.float32),
-            pltpu.VMEM((2, width, width), jnp.float32),
-            pltpu.VMEM((2, groups - 1, part, width), jnp.float32),
-            pltpu.VMEM((2, width, width), jnp.float32),
-            pltpu.VMEM((width, width), jnp.float32),
-            pltpu.VMEM((width, width), jnp.float32),
+            [pltpu.VMEM((groups,) + shape, jnp.float32) for shape in parts],
+            [pltpu.VMEM((groups - 1,) + shape, jnp.float32) for shape in parts],
+            [pltpu.VMEM((groups,) + shape, jnp.float32) for shape in parts],
+            pltpu.VMEM((2, lanes, lanes), jnp.float32),
             pltpu.VMEM(folded, jnp.float32),
             pltpu.VMEM((slices,) + folded, jnp.float32),
             pltpu.SemaphoreType.DMA((steps,)),
@@ -390,10 +395,10 @@
             pltpu.SemaphoreType.DMA((steps,)),
             pltpu.SemaphoreType.DMA((2,)),
             pltpu.SemaphoreType.DMA((2,)),
-            pltpu.SemaphoreType.DMA((2, groups - 1)),
-            pltpu.SemaphoreType.DMA((2, groups - 1)),
-            pltpu.SemaphoreType.DMA((2, groups - 1)),
-            pltpu.SemaphoreType.DMA((2, groups - 1)),
+            pltpu.SemaphoreType.DMA((3, groups - 1)),
+            pltpu.SemaphoreType.DMA((3, groups - 1)),
+            pltpu.SemaphoreType.DMA((3, groups - 1)),
+            pltpu.SemaphoreType.DMA((3, groups - 1)),
             pltpu.SemaphoreType.DMA((slices - 1,)),
             pltpu.SemaphoreType.DMA((slices - 1,)),
         ],

time: 42.3 us -> 40.1 us (0.948)
  Pallas kernels: 37.2 us -> 35 us
    pallas_call x1, Pallas kernels: 37.2 us -> 35 us  [per_device(): pl.pallas_call(functools.partial(kernel, groups, slices), out_shape=(jax....]
where the time goes in v4:
time: 40.1 us; the launch traced here: 40 us
  Pallas kernels  35 us (87%)
  local copies, waits for them, and re-layouts  3.66 us (9%)
  between operations  1.29 us (3%)
    pallas_call x1, Pallas kernels, per_device(): pl.pallas_call(functools.partial(kernel, groups, slices), out_shape=(jax....  35 us
    unnamed x4, local copies, waits for them, and re-layouts  3.66 us

profile of v4, /device:TPU:0, one launch (start us, length us, event | category | flops | bytes accessed | tf_op | source)
XLA Modules:
  0.0 40.0 jit_solution(7281115060191529048)
XLA Ops:
  1.3 35.0 %shard_map.68 = (bf16[4096,256]{1,0:T(8,128)(2,1)}, f32[32,128]{1,0:T(8,128)}) custom-call(bf16[4096,256]{1,0:T(8,128)(2,1)} %psi_hbm.1, f32[32,128]{1,0:T(8,128)} %bitcast.5, f32[32,128]{1,0:T(8,128)} %bitcast.6, s32[1,256]{1,0:T(1,128)} %bitcast.7, s32[1]{0:T(128)S(6)} %copy.9.count_ref), custom_call_target="tpu_custom_call" | custom-call | flops 2147483648 | bytes 2097152 | tf_op jit(solution)/shard_map/pallas_call | solution.py:371
  36.3 0.0 copy-start
  36.3 3.0 %copy.10 = bf16[4096,256]{1,0:T(8,128)(2,1)} copy(bf16[4096,256]{1,0:T(8,128)(2,1)} %get-tuple-element.8) | data formatting | bytes 4194304
  39.3 0.0 copy-done
  39.3 0.6 %copy.11 = f32[4096]{0:T(1024)} copy(f32[4096]{0:T(1024)S(1)} %bitcast.4) | data formatting | bytes 32768
Async XLA Ops:
  36.3 3.1 %copy-start = (f32[32,128]{1,0:T(8,128)S(1)}, f32[32,128]{1,0:T(8,128)}, u32[]{:S(2)}) copy-start(f32[32,128]{1,0:T(8,128)} %get-tuple-element.5) | copy-start | bytes 49156

commit v5 on v4

--- a/solution.py
+++ b/solution.py
@@ -88,16 +88,13 @@
     slices,
     psi_hbm,
     potential_hbm,
-    core_hbm,
     occupation_hbm,
     count_ref,
-    out_hbm,
-    mixed_ref,
+    rotation_ref,
+    density_ref,
     psi,
     potential_ref,
-    core_ref,
     occupation_ref,
-    out,
     applied,
     full,
     partial,
@@ -108,7 +105,6 @@
     shares,
     load_sem,
     small_sem,
-    store_sem,
     halo_send,
     halo_recv,
     scatter_send,
@@ -136,7 +132,6 @@
     small = [
         pltpu.make_async_copy(potential_hbm, potential_ref, small_sem.at[0]),
         pltpu.make_async_copy(occupation_hbm, occupation_ref, small_sem.at[1]),
-        pltpu.make_async_copy(core_hbm, core_ref, small_sem.at[2]),
     ]
     for copy in small:
         copy.start()
@@ -313,14 +308,10 @@
     live = (state < count_ref[0]).astype(jnp.float32)
     weights = occupation_ref[...].astype(jnp.float32) * live / (2.0 * width * slices)
 
-    stores = []
+    rotation_ref[...] = rotation
     for i in range(steps):
         x = psi[pl.ds(halo + i * chunk, chunk), :]
         rotated = jnp.dot(x, rotation, preferred_element_type=jnp.float32)
-        out[pl.ds(i * chunk, chunk), :] = rotated.astype(jnp.bfloat16)
-        here = pl.ds(i * chunk, chunk)
-        stores.append(pltpu.make_async_copy(out.at[here], out_hbm.at[here], store_sem.at[i]))
-        stores[i].start()
         square = rotated * rotated * weights
         narrow = square[:, :lanes]
         for c in range(lanes, width, lanes):
@@ -346,11 +337,57 @@
     shares[cut] = mine[...]
     for copy in copies:
         copy.wait()
-    density = core_ref[...]
-    for c in range(slices):
-        density = density + shares[c]
+    total = shares[0]
+    for c in range(1, slices):
+        total = total + shares[c]
+    density_ref[...] = total
+
+
+def finish(
+    psi_hbm,
+    rotation_hbm,
+    density_hbm,
+    potential_hbm,
+    core_hbm,
+    out_hbm,
+    mixed_ref,
+    psi,
+    rotation,
+    density,
+    potential_ref,
+    core_ref,
+    out,
+    load_sem,
+    small_sem,
+    store_sem,
+):
+    chunk = 4 * lanes
+    pieces = [pl.ds(i * chunk, chunk) for i in range(psi.shape[0] // chunk)]
+    first = pltpu.make_async_copy(rotation_hbm, rotation, small_sem.at[0])
+    first.start()
+    loads = [
+        pltpu.make_async_copy(psi_hbm.at[here], psi.at[here], load_sem.at[i])
+        for i, here in enumerate(pieces)
+    ]
+    small = [
+        pltpu.make_async_copy(density_hbm, density, small_sem.at[1]),
+        pltpu.make_async_copy(potential_hbm, potential_ref, small_sem.at[2]),
+        pltpu.make_async_copy(core_hbm, core_ref, small_sem.at[3]),
+    ]
+    for copy in loads + small:
+        copy.start()
+    first.wait()
+    stores = []
+    for i, here in enumerate(pieces):
+        loads[i].wait()
+        rotated = jnp.dot(psi[here, :], rotation[...], preferred_element_type=jnp.float32)
+        out[here, :] = rotated.astype(jnp.bfloat16)
+        stores.append(pltpu.make_async_copy(out.at[here], out_hbm.at[here], store_sem.at[i]))
+        stores[i].start()
+    for copy in small:
+        copy.wait()
     coefficient = (3.0 / math.pi) ** (1.0 / 3.0)
-    root = jnp.exp(jnp.log(density) * (1.0 / 3.0))
+    root = jnp.exp(jnp.log(core_ref[...] + density[...]) * (1.0 / 3.0))
     mixed_ref[...] = (1.0 - mixing) * potential_ref[...] + mixing * (-coefficient * root)
     for copy in stores:
         copy.wait()
@@ -368,20 +405,19 @@
     ]
     steps = points // (8 * lanes)
     hbm = pl.BlockSpec(memory_space=pltpu.HBM)
-    orbitals_out, potential_out = pl.pallas_call(
+    vmem = pl.BlockSpec(memory_space=pltpu.VMEM)
+    rotation, contribution = pl.pallas_call(
         functools.partial(kernel, groups, slices),
         out_shape=(
-            jax.ShapeDtypeStruct((points, width), jnp.bfloat16),
+            jax.ShapeDtypeStruct((width, width), jnp.bfloat16),
             jax.ShapeDtypeStruct(folded, jnp.float32),
         ),
-        in_specs=[hbm, hbm, hbm, hbm, pl.BlockSpec(memory_space=pltpu.SMEM)],
-        out_specs=(hbm, pl.BlockSpec(memory_space=pltpu.VMEM)),
+        in_specs=[hbm, hbm, hbm, pl.BlockSpec(memory_space=pltpu.SMEM)],
+        out_specs=(vmem, vmem),
         scratch_shapes=[
             pltpu.VMEM((points + 2 * halo, width), jnp.bfloat16),
             pltpu.VMEM(folded, jnp.float32),
-            pltpu.VMEM(folded, jnp.float32),
             pltpu.VMEM((1, width), jnp.int32),
-            pltpu.VMEM((points, width), jnp.bfloat16),
             pltpu.VMEM((8 * lanes, width), jnp.bfloat16),
             pltpu.VMEM((width, width), jnp.float32),
             [pltpu.VMEM((groups,) + shape, jnp.float32) for shape in parts],
@@ -391,8 +427,7 @@
             pltpu.VMEM(folded, jnp.float32),
             pltpu.VMEM((slices,) + folded, jnp.float32),
             pltpu.SemaphoreType.DMA((steps,)),
-            pltpu.SemaphoreType.DMA((3,)),
-            pltpu.SemaphoreType.DMA((steps,)),
+            pltpu.SemaphoreType.DMA((2,)),
             pltpu.SemaphoreType.DMA((2,)),
             pltpu.SemaphoreType.DMA((2,)),
             pltpu.SemaphoreType.DMA((3, groups - 1)),
@@ -411,10 +446,33 @@
     )(
         orbitals,
         potential.reshape(folded),
-        core_density.reshape(folded),
         occupation.reshape(1, width),
         slice_counts,
     )
+    orbitals_out, potential_out = pl.pallas_call(
+        finish,
+        out_shape=(
+            jax.ShapeDtypeStruct((points, width), jnp.bfloat16),
+            jax.ShapeDtypeStruct(folded, jnp.float32),
+        ),
+        in_specs=[hbm] * 5,
+        out_specs=(hbm, vmem),
+        scratch_shapes=[
+            pltpu.VMEM((points, width), jnp.bfloat16),
+            pltpu.VMEM((width, width), jnp.bfloat16),
+            pltpu.VMEM(folded, jnp.float32),
+            pltpu.VMEM(folded, jnp.float32),
+            pltpu.VMEM(folded, jnp.float32),
+            pltpu.VMEM((points, width), jnp.bfloat16),
+            pltpu.SemaphoreType.DMA((points // (4 * lanes),)),
+            pltpu.SemaphoreType.DMA((4,)),
+            pltpu.SemaphoreType.DMA((points // (4 * lanes),)),
+        ],
+        compiler_params=pltpu.CompilerParams(vmem_limit_bytes=60 * 1024 * 1024),
+        cost_estimate=pl.CostEstimate(
+            flops=2 * points * width * width, bytes_accessed=4 * points * width, transcendentals=0
+        ),
+    )(orbitals, rotation, contribution, potential.reshape(folded), core_density.reshape(folded))
     return (orbitals_out, potential_out.reshape(points))
 
 

time: 40.1 us -> 41.4 us (1.032)
  Pallas kernels: 35 us -> 39.9 us
  local copies, waits for them, and re-layouts: 3.66 us -> 0 us
    pallas_call x0 -> x1, Pallas kernels: none -> 4.99 us  [per_device(): pl.pallas_call(finish, out_shape=(jax.ShapeDtypeStruct((points, width), j...]
    unnamed x4 -> x0, local copies, waits for them, and re-layouts: 3.66 us -> none
where the time goes in v5:
time: 41.4 us; the launch traced here: 41.2 us
  Pallas kernels  39.9 us (96%)
  between operations  1.28 us (3%)
    pallas_call x1, Pallas kernels, per_device(): pl.pallas_call(functools.partial(kernel, groups, slices), out_shape=(jax....  34.9 us
    pallas_call x1, Pallas kernels, per_device(): pl.pallas_call(finish, out_shape=(jax.ShapeDtypeStruct((points, width), j...  4.99 us

profile of v5, /device:TPU:0, one launch (start us, length us, event | category | flops | bytes accessed | tf_op | source)
XLA Modules:
  0.0 41.2 jit_solution(15249346990712644124)
XLA Ops:
  1.3 34.9 %shard_map.68 = (bf16[256,256]{1,0:T(8,128)(2,1)}, f32[32,128]{1,0:T(8,128)}) custom-call(bf16[4096,256]{1,0:T(8,128)(2,1)} %psi_hbm.3, f32[32,128]{1,0:T(8,128)} %bitcast.4, s32[1,256]{1,0:T(1,128)} %bitcast.8, s32[1]{0:T(128)S(6)} %copy.7.count_ref), custom_call_target="tpu_custom_call" | custom-call | flops 2147483648 | bytes 2097152 | tf_op jit(solution)/shard_map/pallas_call | solution.py:409
  36.2 5.0 %shard_map.69 = (bf16[4096,256]{1,0:T(8,128)(2,1)}, f32[32,128]{1,0:T(8,128)}) custom-call(bf16[4096,256]{1,0:T(8,128)(2,1)} %psi_hbm.3, bf16[256,256]{1,0:T(8,128)(2,1)} %get-tuple-element.6.rotation_hbm, f32[32,128]{1,0:T(8,128)} %get-tuple-element.7.density_hbm, f32[32,128]{1,0:T(8,128)} %bitcast.5, f32[32,128]{1,0:T(8,128)} %bitcast.6), custom_call_target="tpu_custom_call" | custom-call | flops 536870912 | bytes 4194304 | tf_op jit(solution)/shard_map/pallas_call | solution.py:452

commit v6 on v4

--- a/solution.py
+++ b/solution.py
@@ -6,6 +6,7 @@
 from jax import lax
 from jax.experimental import pallas as pl
 from jax.experimental.pallas import tpu as pltpu
+from jax.experimental.layout import Layout, with_layout_constraint
 from jax.sharding import PartitionSpec as P
 
 mixing = 0.3
@@ -88,16 +89,13 @@
     slices,
     psi_hbm,
     potential_hbm,
-    core_hbm,
     occupation_hbm,
     count_ref,
-    out_hbm,
-    mixed_ref,
+    rotation_ref,
+    density_ref,
     psi,
     potential_ref,
-    core_ref,
     occupation_ref,
-    out,
     applied,
     full,
     partial,
@@ -108,7 +106,6 @@
     shares,
     load_sem,
     small_sem,
-    store_sem,
     halo_send,
     halo_recv,
     scatter_send,
@@ -136,7 +133,6 @@
     small = [
         pltpu.make_async_copy(potential_hbm, potential_ref, small_sem.at[0]),
         pltpu.make_async_copy(occupation_hbm, occupation_ref, small_sem.at[1]),
-        pltpu.make_async_copy(core_hbm, core_ref, small_sem.at[2]),
     ]
     for copy in small:
         copy.start()
@@ -313,14 +309,10 @@
     live = (state < count_ref[0]).astype(jnp.float32)
     weights = occupation_ref[...].astype(jnp.float32) * live / (2.0 * width * slices)
 
-    stores = []
+    rotation_ref[...] = rotation
     for i in range(steps):
         x = psi[pl.ds(halo + i * chunk, chunk), :]
         rotated = jnp.dot(x, rotation, preferred_element_type=jnp.float32)
-        out[pl.ds(i * chunk, chunk), :] = rotated.astype(jnp.bfloat16)
-        here = pl.ds(i * chunk, chunk)
-        stores.append(pltpu.make_async_copy(out.at[here], out_hbm.at[here], store_sem.at[i]))
-        stores[i].start()
         square = rotated * rotated * weights
         narrow = square[:, :lanes]
         for c in range(lanes, width, lanes):
@@ -346,14 +338,10 @@
     shares[cut] = mine[...]
     for copy in copies:
         copy.wait()
-    density = core_ref[...]
-    for c in range(slices):
-        density = density + shares[c]
-    coefficient = (3.0 / math.pi) ** (1.0 / 3.0)
-    root = jnp.exp(jnp.log(density) * (1.0 / 3.0))
-    mixed_ref[...] = (1.0 - mixing) * potential_ref[...] + mixing * (-coefficient * root)
-    for copy in stores:
-        copy.wait()
+    total = shares[0]
+    for c in range(1, slices):
+        total = total + shares[c]
+    density_ref[...] = total
 
 
 def per_device(orbitals, potential, core_density, occupation, slice_counts):
@@ -368,20 +356,19 @@
     ]
     steps = points // (8 * lanes)
     hbm = pl.BlockSpec(memory_space=pltpu.HBM)
-    orbitals_out, potential_out = pl.pallas_call(
+    vmem = pl.BlockSpec(memory_space=pltpu.VMEM)
+    rotation, contribution = pl.pallas_call(
         functools.partial(kernel, groups, slices),
         out_shape=(
-            jax.ShapeDtypeStruct((points, width), jnp.bfloat16),
+            jax.ShapeDtypeStruct((width, width), jnp.bfloat16),
             jax.ShapeDtypeStruct(folded, jnp.float32),
         ),
-        in_specs=[hbm, hbm, hbm, hbm, pl.BlockSpec(memory_space=pltpu.SMEM)],
-        out_specs=(hbm, pl.BlockSpec(memory_space=pltpu.VMEM)),
+        in_specs=[hbm, hbm, hbm, pl.BlockSpec(memory_space=pltpu.SMEM)],
+        out_specs=(vmem, vmem),
         scratch_shapes=[
             pltpu.VMEM((points + 2 * halo, width), jnp.bfloat16),
             pltpu.VMEM(folded, jnp.float32),
-            pltpu.VMEM(folded, jnp.float32),
             pltpu.VMEM((1, width), jnp.int32),
-            pltpu.VMEM((points, width), jnp.bfloat16),
             pltpu.VMEM((8 * lanes, width), jnp.bfloat16),
             pltpu.VMEM((width, width), jnp.float32),
             [pltpu.VMEM((groups,) + shape, jnp.float32) for shape in parts],
@@ -391,8 +378,7 @@
             pltpu.VMEM(folded, jnp.float32),
             pltpu.VMEM((slices,) + folded, jnp.float32),
             pltpu.SemaphoreType.DMA((steps,)),
-            pltpu.SemaphoreType.DMA((3,)),
-            pltpu.SemaphoreType.DMA((steps,)),
+            pltpu.SemaphoreType.DMA((2,)),
             pltpu.SemaphoreType.DMA((2,)),
             pltpu.SemaphoreType.DMA((2,)),
             pltpu.SemaphoreType.DMA((3, groups - 1)),
@@ -411,11 +397,16 @@
     )(
         orbitals,
         potential.reshape(folded),
-        core_density.reshape(folded),
         occupation.reshape(1, width),
         slice_counts,
     )
-    return (orbitals_out, potential_out.reshape(points))
+    rotated = jnp.dot(orbitals, rotation, preferred_element_type=jnp.float32)
+    rotated = with_layout_constraint(rotated, Layout(major_to_minor=(0, 1)))
+    orbitals_out = rotated.astype(jnp.bfloat16)
+    coefficient = (3.0 / math.pi) ** (1.0 / 3.0)
+    density = core_density + contribution.reshape(points)
+    potential_out = (1.0 - mixing) * potential + mixing * (-coefficient * jnp.cbrt(density))
+    return (orbitals_out, potential_out)
 
 
 def solution(mesh):

time: 40.1 us -> 40.9 us (1.020)
  local copies, waits for them, and re-layouts: 3.66 us -> 0.01 us
  matrix products: 0 us -> 2.93 us
  other arithmetic: 0 us -> 1.35 us
    unnamed x4 -> x6, local copies, waits for them, and re-layouts: 3.66 us -> 0.01 us
    dot_general x0 -> x1, matrix products: none -> 2.93 us  [per_device(): rotated = jnp.dot(orbitals, rotation, preferred_element_type=jnp.float32)]
    add x0 -> x1, other arithmetic: none -> 1.35 us  [per_device(): (1.0 - mixing) * potential + mixing * (-coefficient * jnp.cbrt(density))]
where the time goes in v6:
time: 40.9 us; the launch traced here: 40.7 us
  Pallas kernels  35.1 us (86%)
  matrix products  2.93 us (7%)
  other arithmetic  1.35 us (3%)
  between operations  1.33 us (3%)
    pallas_call x1, Pallas kernels, per_device(): pl.pallas_call(functools.partial(kernel, groups, slices), out_shape=(jax....  35.1 us
    dot_general x1, matrix products, per_device(): rotated = jnp.dot(orbitals, rotation, preferred_element_type=jnp.float32)  2.93 us
    add x1, other arithmetic, per_device(): (1.0 - mixing) * potential + mixing * (-coefficient * jnp.cbrt(density))  1.35 us

profile of v6, /device:TPU:0, one launch (start us, length us, event | category | flops | bytes accessed | tf_op | source)
XLA Modules:
  0.0 40.7 jit_solution(7104754362639518343)
XLA Ops:
  1.3 0.0 copy-start.1
  1.3 0.0 copy-start.2
  1.3 0.0 copy-start
  1.3 35.1 %shard_map.68 = (bf16[256,256]{1,0:T(8,128)(2,1)}, f32[32,128]{1,0:T(8,128)}) custom-call(bf16[4096,256]{1,0:T(8,128)(2,1)} %psi_hbm.1, f32[32,128]{1,0:T(8,128)} %bitcast.16, s32[1,256]{1,0:T(1,128)} %bitcast.17, s32[1]{0:T(128)S(6)} %copy.7.count_ref), custom_call_target="tpu_custom_call" | custom-call | flops 2147483648 | bytes 2097152 | tf_op jit(solution)/shard_map/pallas_call | solution.py:360
  36.4 0.0 copy-done.1
  36.4 0.0 copy-done.2
  36.4 1.4 %fusion.3 = f32[4096]{0:T(1024)} fusion(f32[4096]{0:T(1024)S(1)} %copy-done.2, f32[32,128]{1,0:T(8,128)} %get-tuple-element.5, f32[4096]{0:T(1024)S(1)} %copy-done.1), kind=kLoop, calls=%fused_computation.5 | loop fusion | flops 16384 | bytes 65536 | tf_op jit(solution)/shard_map/add | solution.py:408
  37.8 0.0 copy-done
  37.8 2.9 %fusion = bf16[4096,256]{1,0:T(8,128)(2,1)} fusion(bf16[4096,256]{1,0:T(8,128)(2,1)S(1)} %copy-done, bf16[256,256]{1,0:T(8,128)(2,1)} %get-tuple-element.4), kind=kOutput, calls=%fused_computation.1 | convolution fusion | flops 537919488 | bytes 4325376 | tf_op jit(solution)/shard_map/dot_general | solution.py:403
Async XLA Ops:
  1.3 35.1 %copy-start.1 = (f32[4096]{0:T(1024)S(1)}, f32[4096]{0:T(1024)}, u32[]{:S(2)}) copy-start(f32[4096]{0:T(1024)} %param.6) | copy-start | bytes 49156
  1.3 35.1 %copy-start.2 = (f32[4096]{0:T(1024)S(1)}, f32[4096]{0:T(1024)}, u32[]{:S(2)}) copy-start(f32[4096]{0:T(1024)} %param.7) | copy-start | bytes 49156
  1.3 36.5 %copy-start = (bf16[4096,256]{1,0:T(8,128)(2,1)S(1)}, bf16[4096,256]{1,0:T(8,128)(2,1)}, u32[]{:S(2)}) copy-start(bf16[4096,256]{1,0:T(8,128)(2,1)} %psi_hbm.1) | copy-start | bytes 6291460

commit v7 on v4

--- a/solution.py
+++ b/solution.py
@@ -291,9 +291,9 @@
         )
 
     lead = factorise(collect(0, first), factors.at[0])
+    third = gather(2, third)
     rest = collect(1, second)
     coupled = exact(lead, rest[:lanes], along)
-    third = gather(2, third)
     tail = factorise(rest[lanes:] - exact(coupled, coupled, columns), factors.at[1])
     corner = exact(tail, exact(coupled, lead, columns), along)
     inverse = jnp.concatenate(

time: 40.1 us -> 40.7 us (1.015)
  Pallas kernels: 35 us -> 35.6 us
    pallas_call x1, Pallas kernels: 35 us -> 35.6 us  [per_device(): pl.pallas_call(functools.partial(kernel, groups, slices), out_shape=(jax....]
where the time goes in v7:
time: 40.7 us; the launch traced here: 40.5 us
  Pallas kernels  35.6 us (87%)
  local copies, waits for them, and re-layouts  3.66 us (9%)
  between operations  1.29 us (3%)
    pallas_call x1, Pallas kernels, per_device(): pl.pallas_call(functools.partial(kernel, groups, slices), out_shape=(jax....  35.6 us
    unnamed x4, local copies, waits for them, and re-layouts  3.66 us

profile of v7, /device:TPU:0, one launch (start us, length us, event | category | flops | bytes accessed | tf_op | source)
XLA Modules:
  0.0 40.5 jit_solution(16920275029063403057)
XLA Ops:
  1.3 35.6 %shard_map.68 = (bf16[4096,256]{1,0:T(8,128)(2,1)}, f32[32,128]{1,0:T(8,128)}) custom-call(bf16[4096,256]{1,0:T(8,128)(2,1)} %psi_hbm.1, f32[32,128]{1,0:T(8,128)} %bitcast.5, f32[32,128]{1,0:T(8,128)} %bitcast.6, s32[1,256]{1,0:T(1,128)} %bitcast.7, s32[1]{0:T(128)S(6)} %copy.9.count_ref), custom_call_target="tpu_custom_call" | custom-call | flops 2147483648 | bytes 2097152 | tf_op jit(solution)/shard_map/pallas_call | solution.py:371
  36.9 0.0 copy-start
  36.9 3.0 %copy.10 = bf16[4096,256]{1,0:T(8,128)(2,1)} copy(bf16[4096,256]{1,0:T(8,128)(2,1)} %get-tuple-element.8) | data formatting | bytes 4194304
  39.9 0.0 copy-done
  39.9 0.6 %copy.11 = f32[4096]{0:T(1024)} copy(f32[4096]{0:T(1024)S(1)} %bitcast.4) | data formatting | bytes 32768
Async XLA Ops:
  36.9 3.1 %copy-start = (f32[32,128]{1,0:T(8,128)S(1)}, f32[32,128]{1,0:T(8,128)}, u32[]{:S(2)}) copy-start(f32[32,128]{1,0:T(8,128)} %get-tuple-element.5) | copy-start | bytes 49156
